TPU v7x, 128 devices: a whole 4x4x4 slice. The times are simulated.
128 devices in a mesh: seq: 8 (over z_hi, y), ctx: 16 (over z_lo, x, core).
Axes of the slice: x: 4, y: 4, z: 4 (z_hi: 2, z_lo: 2; z = z_hi * 2 + z_lo), core: 2. Of those that a mesh axis runs over, the one named last changes fastest.
Arguments:
- queries: bfloat16 [8, 2048, 4096], P('seq', 'ctx'), may hold values from -6 to 6
- keys_in: bfloat16 [8, 2048, 4096], P('seq', 'ctx'), may hold values from -6 to 6
- value_in: bfloat16 [8, 2048, 4096], P('seq', 'ctx'), may hold values from -6 to 6
- upstream: bfloat16 [8, 2048, 4096], P('seq', 'ctx'), may hold values from -6 to 6
- filter_taps: float32 [2048, 4096], P(None, 'ctx'), may hold values from -0.125 to 0.125
Outputs:
- query_grad: bfloat16 [8, 2048, 4096], P('seq', 'ctx')
- key_grad: bfloat16 [8, 2048, 4096], P('seq', 'ctx')
- value_grad: bfloat16 [8, 2048, 4096], P('seq', 'ctx')
- filter_grad: float32 [2048, 4096], P(None, 'ctx')
All inputs are finite; a program needn't handle non-finite values.
Results may differ from a plain program's by a relative error of at most 0.009.
Values may be sent and summed in bfloat16 or wider, within the bound.
No kernel may reach another device: no remote copies, remote signals or barrier semaphores. Data moves between devices by JAX's collectives and lax.ppermute only.
A program may use at most 192 MiB of HBM per device.

v0:
```python
import functools
import math

import jax
import jax.numpy as jnp
import numpy as np
from jax import lax
from jax.experimental import pallas as pl
from jax.experimental.pallas import tpu as pltpu
from jax.sharding import PartitionSpec as P

BLOCK = 256
HALF = 64
LANES = 128
F32 = jnp.float32
BF16 = jnp.bfloat16
VMEM_LIMIT = 48 * 1024 * 1024


def dft_tables():
    freq = np.arange(BLOCK)[:, None] * 2 + 1
    time = np.arange(BLOCK)[None, :]
    angle = (freq * time % (4 * BLOCK)) * (2.0 * math.pi / (4 * BLOCK))
    forward = np.concatenate((np.cos(angle), -np.sin(angle)), axis=0).astype(np.float32)
    upper = forward.astype(jnp.bfloat16)
    lower = (forward - upper.astype(np.float32)).astype(jnp.bfloat16)
    inverse = (forward.T / BLOCK).astype(jnp.bfloat16)
    return upper, lower, inverse


def low_lanes(shape):
    return lax.broadcasted_iota(jnp.int32, shape, len(shape) - 1) < HALF


def swap_halves(first, second):
    mask = low_lanes(first.shape)
    return (
        jnp.where(mask, first, pltpu.roll(second, HALF, 1)),
        jnp.where(mask, pltpu.roll(first, HALF, 1), second),
    )


def row_signs(shape):
    row = lax.broadcasted_iota(jnp.int32, shape, 0)
    return (1 - 2 * (row % 2)).astype(F32)


def gate_kernel(q_ref, k_ref, v_ref, u_ref, out_ref):
    blocks = out_ref.shape[1]
    half_rows = out_ref.shape[3]
    for block in range(blocks):
        for pair in range(2):
            lanes = pl.ds((block * 2 + pair) * LANES, LANES)
            kv = k_ref[:, lanes].astype(F32) * v_ref[:, lanes].astype(F32)
            gg = u_ref[:, lanes].astype(F32) * q_ref[:, lanes].astype(F32)
            for signal, value in enumerate((kv, gg)):
                even, odd = swap_halves(value[:half_rows], value[half_rows:])
                out_ref[2 * pair, block, signal] = even.astype(BF16)
                out_ref[2 * pair + 1, block, signal] = odd.astype(BF16)


def filter_kernel(place_ref, taps_ref, upper_ref, lower_ref, out_ref):
    blocks = out_ref.shape[0]
    odd = place_ref[0] % 2
    signs = row_signs((BLOCK, LANES))
    mask = low_lanes((BLOCK, LANES))
    before = None
    for block in range(blocks):
        taps = taps_ref[pl.ds(block * BLOCK, BLOCK), :]
        turned = pltpu.roll(taps, HALF, 1)
        taps = jnp.where(jnp.logical_xor(mask, odd == 1), taps, turned)
        high = taps.astype(BF16)
        low = (taps - high.astype(F32)).astype(BF16)
        spec = jnp.dot(upper_ref[...], high, preferred_element_type=F32)
        spec = spec + jnp.dot(upper_ref[...], low, preferred_element_type=F32)
        spec = spec + jnp.dot(lower_ref[...], high, preferred_element_type=F32)
        real, imag = spec[:BLOCK], spec[BLOCK:]
        if before is None:
            out_ref[block, :BLOCK] = real
            out_ref[block, BLOCK:] = imag
        else:
            out_ref[block, :BLOCK] = real - signs * before[1]
            out_ref[block, BLOCK:] = imag + signs * before[0]
        before = (real, imag)


def conv_kernel(
    arrived_ref, filt_ref, forward_ref, inverse_ref, out_ref, grad_ref, sig_ref, spec_ref, prod_ref
):
    blocks = filt_ref.shape[0]
    slots = arrived_ref.shape[1]
    half_rows = arrived_ref.shape[3]
    per_block = slots // blocks
    for signal in range(2):
        for slot in range(slots):
            for pair in range(2):
                lanes = pl.ds(pair * LANES, LANES)
                first, second = swap_halves(
                    arrived_ref[2 * pair, slot, signal].astype(F32),
                    arrived_ref[2 * pair + 1, slot, signal].astype(F32),
                )
                at = (slot % per_block) * 2 * half_rows
                sig_ref[signal, slot // per_block, pl.ds(at, half_rows), lanes] = first.astype(BF16)
                sig_ref[signal, slot // per_block, pl.ds(at + half_rows, half_rows), lanes] = (
                    second.astype(BF16)
                )
    for signal in range(2):
        for block in range(blocks):
            spec_ref[signal, block] = jnp.dot(
                forward_ref[...], sig_ref[signal, block], preferred_element_type=F32
            )

    rows_at_once = 16
    signs = row_signs((rows_at_once, LANES))

    def tile(step, carry):
        row = pl.multiple_of((step // 2) * rows_at_once, rows_at_once)
        real_rows = pl.ds(row, rows_at_once)
        imag_rows = pl.ds(BLOCK + row, rows_at_once)
        lanes = pl.ds(pl.multiple_of((step % 2) * LANES, LANES), LANES)
        filt = [(filt_ref[b, real_rows, :], filt_ref[b, imag_rows, :]) for b in range(blocks)]
        value = [
            (spec_ref[0, b, real_rows, lanes], spec_ref[0, b, imag_rows, lanes]) for b in range(blocks)
        ]
        grad = [
            (spec_ref[1, b, real_rows, lanes], spec_ref[1, b, imag_rows, lanes]) for b in range(blocks)
        ]
        window = []
        for b in range(blocks):
            if b + 1 < blocks:
                window.append(
                    (grad[b][0] + signs * grad[b + 1][1], grad[b][1] - signs * grad[b + 1][0])
                )
            else:
                window.append(grad[b])

        def store(kind, block, real, imag):
            prod_ref[kind, block, real_rows, lanes] = real.astype(BF16)
            prod_ref[kind, block, imag_rows, lanes] = imag.astype(BF16)

        def total(terms):
            out = None
            for term in terms:
                out = term if out is None else out + term
            return out

        for b in range(blocks):
            pairs = [(filt[j], value[b - j]) for j in range(b + 1)]
            store(
                0,
                b,
                total([h[0] * x[0] - h[1] * x[1] for h, x in pairs]),
                total([h[0] * x[1] + h[1] * x[0] for h, x in pairs]),
            )
        for b in range(blocks):
            pairs = [(filt[j], grad[b + j]) for j in range(blocks - b)]
            store(
                1,
                b,
                total([h[0] * x[0] + h[1] * x[1] for h, x in pairs]),
                total([h[0] * x[1] - h[1] * x[0] for h, x in pairs]),
            )
        for b in range(blocks):
            pairs = [(value[j], window[b + j]) for j in range(blocks - b)]
            store(
                2,
                b,
                total([h[0] * x[0] + h[1] * x[1] for h, x in pairs]),
                total([h[0] * x[1] - h[1] * x[0] for h, x in pairs]),
            )
        return carry

    lax.fori_loop(0, BLOCK // rows_at_once * 2, tile, 0)

    mask = low_lanes((BLOCK, LANES))
    folded = []
    for block in range(blocks):
        cross = jnp.dot(inverse_ref[...], prod_ref[2, block], preferred_element_type=F32)
        cross = cross[:, :LANES] + cross[:, LANES:]
        folded.append(cross + pltpu.roll(cross, HALF, 1))
        if block >= blocks // 2:
            at = block - blocks // 2
            grad_ref[pl.ds(at * BLOCK, BLOCK), :] = jnp.where(
                mask, folded[at], folded[block]
            ).astype(BF16)
    for signal in range(2):
        for block in range(blocks):
            result = jnp.dot(inverse_ref[...], prod_ref[signal, block], preferred_element_type=F32)
            for part in range(per_block):
                for pair in range(2):
                    at = part * 2 * half_rows
                    lanes = slice(pair * LANES, (pair + 1) * LANES)
                    even, odd = swap_halves(
                        result[at : at + half_rows, lanes],
                        result[at + half_rows : at + 2 * half_rows, lanes],
                    )
                    slot = block * per_block + part
                    out_ref[2 * pair, slot, signal] = even.astype(BF16)
                    out_ref[2 * pair + 1, slot, signal] = odd.astype(BF16)


def final_kernel(ret_ref, k_ref, v_ref, u_ref, dq_ref, dk_ref, dv_ref):
    blocks = ret_ref.shape[1]
    half_rows = ret_ref.shape[3]
    for block in range(blocks):
        for pair in range(2):
            lanes = pl.ds((block * 2 + pair) * LANES, LANES)
            conv = swap_halves(
                ret_ref[2 * pair, block, 0].astype(F32), ret_ref[2 * pair + 1, block, 0].astype(F32)
            )
            back = swap_halves(
                ret_ref[2 * pair, block, 1].astype(F32), ret_ref[2 * pair + 1, block, 1].astype(F32)
            )
            for part in range(2):
                rows = pl.ds(part * half_rows, half_rows)
                dq_ref[rows, lanes] = (u_ref[rows, lanes].astype(F32) * conv[part]).astype(BF16)
                dk_ref[rows, lanes] = (back[part] * v_ref[rows, lanes].astype(F32)).astype(BF16)
                dv_ref[rows, lanes] = (back[part] * k_ref[rows, lanes].astype(F32)).astype(BF16)


def spread_kernel(gathered_ref, out_ref, *, scale):
    rows = gathered_ref.shape[1]
    for pair in range(2):
        lanes = pl.ds(pair * LANES, LANES)
        first, second = swap_halves(
            gathered_ref[2 * pair].astype(F32) * scale, gathered_ref[2 * pair + 1].astype(F32) * scale
        )
        out_ref[pl.ds(0, rows), lanes] = first
        out_ref[pl.ds(rows, rows), lanes] = second


def local(queries, keys_in, value_in, upstream, filter_taps, *, ctx_count, seq_count):
    tokens, channels = queries.shape[1], queries.shape[2]
    length = filter_taps.shape[0]
    blocks = length // BLOCK
    y_count = 4
    z_count = seq_count // y_count
    half_rows = tokens // 2
    q2, k2, v2, u2 = (a.reshape(tokens, channels) for a in (queries, keys_in, value_in, upstream))
    params = pltpu.CompilerParams(vmem_limit_bytes=VMEM_LIMIT)
    upper, lower, inverse = (jnp.asarray(t) for t in dft_tables())
    groups = [
        [(z * y_count + y) * ctx_count + c for y in range(y_count) for c in range(ctx_count)]
        for z in range(z_count)
    ]

    steps = 4
    part = ctx_count // steps
    gate_in = pl.BlockSpec((tokens, part * BLOCK), lambda i: (0, i))
    packed_spec = pl.BlockSpec((y_count, part, 2, half_rows, LANES), lambda i: (0, i, 0, 0, 0))
    packed_shape = jax.ShapeDtypeStruct((y_count, ctx_count, 2, half_rows, LANES), BF16)
    packed = pl.pallas_call(
        gate_kernel,
        grid=(steps,),
        in_specs=[gate_in] * 4,
        out_specs=packed_spec,
        out_shape=packed_shape,
        compiler_params=params,
        name="gate",
    )(q2, k2, v2, u2)

    def exchange(array):
        flat = array.reshape((y_count * ctx_count,) + array.shape[2:])
        moved = lax.all_to_all(flat, ("seq", "ctx"), 0, 0, tiled=True, axis_index_groups=groups)
        return moved.reshape(array.shape)

    arrived = exchange(packed)

    place = lax.rem(lax.axis_index("seq"), y_count).astype(jnp.int32).reshape(1)
    filt = pl.pallas_call(
        filter_kernel,
        grid_spec=pltpu.PrefetchScalarGridSpec(
            num_scalar_prefetch=1,
            grid=(1,),
            in_specs=[
                pl.BlockSpec((length, LANES), lambda i, place: (0, place[0] // 2)),
                pl.BlockSpec((2 * BLOCK, BLOCK), lambda i, place: (0, 0)),
                pl.BlockSpec((2 * BLOCK, BLOCK), lambda i, place: (0, 0)),
            ],
            out_specs=pl.BlockSpec((blocks, 2 * BLOCK, LANES), lambda i, place: (0, 0, 0)),
        ),
        out_shape=jax.ShapeDtypeStruct((blocks, 2 * BLOCK, LANES), F32),
        compiler_params=params,
        name="filter_spectra",
    )(place, filter_taps, upper, lower)

    whole = pl.BlockSpec(memory_space=pltpu.VMEM)
    outgoing, part_grad = pl.pallas_call(
        conv_kernel,
        in_specs=[whole] * 4,
        out_specs=[whole] * 2,
        out_shape=[packed_shape, jax.ShapeDtypeStruct((length // 2, LANES), BF16)],
        scratch_shapes=[
            pltpu.VMEM((2, blocks, BLOCK, 2 * LANES), BF16),
            pltpu.VMEM((2, blocks, 2 * BLOCK, 2 * LANES), F32),
            pltpu.VMEM((3, blocks, 2 * BLOCK, 2 * LANES), BF16),
        ],
        compiler_params=params,
        name="convolve",
    )(arrived, filt, upper, inverse)

    swapped = lax.ppermute(
        part_grad, "seq", [(s, (s + y_count) % seq_count) for s in range(seq_count)]
    )
    returned = exchange(outgoing)
    summed = (part_grad.astype(F32) + swapped.astype(F32)).astype(BF16)
    gathered = lax.all_gather(
        summed,
        "seq",
        axis=0,
        tiled=False,
        axis_index_groups=[[z * y_count + y for y in range(y_count)] for z in range(z_count)],
    )

    shape = jax.ShapeDtypeStruct((tokens, channels), BF16)
    query_grad, key_grad, value_grad = pl.pallas_call(
        final_kernel,
        grid=(steps,),
        in_specs=[packed_spec] + [gate_in] * 3,
        out_specs=[gate_in] * 3,
        out_shape=[shape] * 3,
        compiler_params=params,
        name="products",
    )(returned, k2, v2, u2)

    filter_grad = pl.pallas_call(
        functools.partial(spread_kernel, scale=1.0 / math.sqrt(length * seq_count)),
        in_specs=[whole],
        out_specs=whole,
        out_shape=jax.ShapeDtypeStruct((length, 2 * LANES), F32),
        compiler_params=params,
        name="spread",
    )(gathered)
    return (
        query_grad.reshape(queries.shape),
        key_grad.reshape(queries.shape),
        value_grad.reshape(queries.shape),
        filter_grad,
    )


def solution(mesh):
    return jax.shard_map(
        functools.partial(local, ctx_count=mesh.shape["ctx"], seq_count=mesh.shape["seq"]),
        mesh=mesh,
        in_specs=(
            P("seq", "ctx", None),
            P("seq", "ctx", None),
            P("seq", "ctx", None),
            P("seq", "ctx", None),
            P(None, "ctx"),
        ),
        out_specs=(
            P("seq", "ctx", None),
            P("seq", "ctx", None),
            P("seq", "ctx", None),
            P(None, "ctx"),
        ),
        check_vma=False,
    )
```

profile of v0, /device:TPU:1, one launch (start us, length us, event | category | flops | bytes accessed | tf_op | source)
XLA Modules:
  0.0 128.8 jit_solution(6819449925791447789)
XLA Ops:
  7.2 0.0 copy-start.1
  7.2 1.2 copy-done.1
  8.4 0.0 copy-start.3
  8.4 1.2 copy-done.3
  9.6 0.0 copy-start.5
  9.6 1.2 copy-done.5
  10.8 0.0 copy-start.11
  10.8 1.2 copy-done.11
  12.1 2.7 %gate.1 = bf16[4,16,2,64,128]{4,3,2,1,0:T(8,128)(2,1)} custom-call(bf16[128,4096]{1,0:T(8,128)(2,1)S(1)} %bitcast.23, bf16[128,4096]{1,0:T(8,128)(2,1)S(1)} %bitcast.15, bf16[128,4096]{1,0:T(8,128)(2,1)S(1)} %bitcast.17, bf16[128,4096]{1,0:T(8,128)(2,1)S(1)} %bitcast.19), custom_call_target="tpu_custom_call" | custom-call | tf_op jit(solution)/shard_map/gate/pallas_call | solution.py:252
  14.7 0.0 copy-start.10
  14.7 0.0 copy-start.13
  14.7 10.5 %all-to-all-start = ((bf16[64,2,64,128]{3,2,1,0:T(8,128)(2,1)}), bf16[64,2,64,128]{3,2,1,0:T(8,128)(2,1)S(1)}, u32[]{:S(2)}, u32[]{:S(2)}) async-start(bf16[64,2,64,128]{3,2,1,0:T(8,128)(2,1)} %bitcast.24), calls=%async_computation | async-start | bytes 4194304 | tf_op jit(solution)/shard_map/all_to_all | solution.py:264
  25.2 0.0 copy-done.10
  25.2 0.0 copy-done.13
  25.3 0.0 copy-start.7
  25.3 1.6 %copy-done.7 = f32[2048,256]{1,0:T(8,128)S(1)} copy-done((f32[2048,256]{1,0:T(8,128)S(1)}, f32[2048,256]{1,0:T(8,128)}, u32[]{:S(2)}) %copy-start.7) | copy-done | bytes 2097176
  26.8 0.0 copy-start.12
  26.8 1.9 %filter_spectra.1.filt_ref = f32[8,512,128]{2,1,0:T(8,128)S(1)} custom-call(s32[1]{0:T(128)} %bitcast.6.place_ref, f32[2048,256]{1,0:T(8,128)S(1)} %copy-done.7, bf16[512,256]{1,0:T(8,128)(2,1)S(1)} %copy-done.10, bf16[512,256]{1,0:T(8,128)(2,1)S(1)} %copy-done.13), custom_call_target="tpu_custom_call" | custom-call | tf_op jit(solution)/shard_map/filter_spectra/pallas_call | solution.py:270
  28.8 0.0 copy-start
  28.8 1.3 %copy-done = f32[8,512,128]{2,1,0:T(8,128)} copy-done((f32[8,512,128]{2,1,0:T(8,128)}, f32[8,512,128]{2,1,0:T(8,128)S(1)}, u32[]{:S(2)}) %copy-start) | copy-done | bytes 2097176
  30.1 24.5 %all-to-all-done = bf16[64,2,64,128]{3,2,1,0:T(8,128)(2,1)S(1)} async-done(((bf16[64,2,64,128]{3,2,1,0:T(8,128)(2,1)}), bf16[64,2,64,128]{3,2,1,0:T(8,128)(2,1)S(1)}, u32[]{:S(2)}, u32[]{:S(2)}) %all-to-all-start) | async-done | bytes 2097184 | tf_op jit(solution)/shard_map/all_to_all | solution.py:264
  54.6 0.0 copy-done.12
  54.6 13.8 %convolve.1 = (bf16[4,16,2,64,128]{4,3,2,1,0:T(8,128)(2,1)S(1)}, bf16[1024,128]{1,0:T(8,128)(2,1)S(1)}) custom-call(bf16[4,16,2,64,128]{4,3,2,1,0:T(8,128)(2,1)S(1)} %bitcast.13, f32[8,512,128]{2,1,0:T(8,128)} %copy-done, bf16[512,256]{1,0:T(8,128)(2,1)S(1)} %copy-done.10, bf16[256,512]{1,0:T(8,128)(2,1)S(1)} %copy-done.12), custom_call_target="tpu_custom_call" | custom-call | tf_op jit(solution)/shard_map/convolve/pallas_call | solution.py:288
  68.4 0.0 copy-start.8
  68.4 1.3 %copy-done.8 = bf16[4,16,2,64,128]{4,3,2,1,0:T(8,128)(2,1)} copy-done((bf16[4,16,2,64,128]{4,3,2,1,0:T(8,128)(2,1)}, bf16[4,16,2,64,128]{4,3,2,1,0:T(8,128)(2,1)S(1)}, u32[]{:S(2)}) %copy-start.8) | copy-done | bytes 2097176
  69.7 3.3 %collective-permute-start = (bf16[1024,128]{1,0:T(8,128)(2,1)S(1)}, bf16[1024,128]{1,0:T(8,128)(2,1)}, u32[]{:S(2)}, u32[]{:S(2)}) collective-permute-start(bf16[1024,128]{1,0:T(8,128)(2,1)S(1)} %get-tuple-element.13), channel_id=1, source_target_pairs={{0,64},{16,80},{32,96},{48,112},{64,0},{80,16},{96,32},{112,48},{1... | collective-permute-start | bytes 786440 | tf_op jit(solution)/shard_map/ppermute | solution.py:302
  73.0 4.9 %all-to-all-start.1 = ((bf16[64,2,64,128]{3,2,1,0:T(8,128)(2,1)}), bf16[64,2,64,128]{3,2,1,0:T(8,128)(2,1)S(1)}, u32[]{:S(2)}, u32[]{:S(2)}) async-start(bf16[64,2,64,128]{3,2,1,0:T(8,128)(2,1)} %bitcast.21), calls=%async_computation.1 | async-start | bytes 4194304 | tf_op jit(solution)/shard_map/all_to_all | solution.py:264
  77.9 0.0 copy-start.2
  78.0 0.0 all-gather.3.cloned.1.call-start
  78.0 1.7 %collective-permute-done = bf16[1024,128]{1,0:T(8,128)(2,1)} collective-permute-done((bf16[1024,128]{1,0:T(8,128)(2,1)S(1)}, bf16[1024,128]{1,0:T(8,128)(2,1)}, u32[]{:S(2)}, u32[]{:S(2)}) %collective-permute-start) | collective-permute-done | bytes 262176 | tf_op jit(solution)/shard_map/ppermute | solution.py:302
  79.7 1.7 %add_convert_fusion = bf16[1024,128]{1,0:T(8,128)(2,1)} fusion(bf16[1024,128]{1,0:T(8,128)(2,1)} %collective-permute-done, bf16[1024,128]{1,0:T(8,128)(2,1)S(1)} %get-tuple-element.13), kind=kLoop, calls=%fused_computation | loop fusion | flops 524288 | bytes 786432 | tf_op jit(solution)/shard_map/convert_element_type | solution.py:306
  81.4 0.0 all-gather.3.cloned.1.call-update
  81.5 31.8 %all-gather.3.cloned.1.call-done = bf16[4096,128]{1,0:T(8,128)(2,1)} async-done(((bf16[1024,128]{1,0:T(8,128)(2,1)}), bf16[4096,128]{1,0:T(8,128)(2,1)}) %all-gather.3.cloned.1.call-update) | async-done | bytes 1048592 | tf_op jit(solution)/shard_map/all_gather | solution.py:307
  113.2 0.0 copy-start.9
  113.2 1.2 copy-done.9
  114.4 1.9 %spread.1 = f32[2048,256]{1,0:T(8,128)} custom-call(bf16[4,1024,128]{2,1,0:T(8,128)(2,1)S(1)} %bitcast.22), custom_call_target="tpu_custom_call" | custom-call | tf_op jit(solution)/shard_map/spread/pallas_call | solution.py:326
  116.4 0.0 all-to-all-done.1
  116.4 0.0 copy-done.2
  116.4 0.0 copy-start.4
  116.4 1.2 copy-done.4
  117.6 0.0 copy-start.6
  117.6 1.2 copy-done.6
  118.8 3.2 %products.1 = (bf16[128,4096]{1,0:T(8,128)(2,1)}, bf16[128,4096]{1,0:T(8,128)(2,1)}, bf16[128,4096]{1,0:T(8,128)(2,1)}) custom-call(bf16[4,16,2,64,128]{4,3,2,1,0:T(8,128)(2,1)S(1)} %bitcast.14, bf16[128,4096]{1,0:T(8,128)(2,1)S(1)} %bitcast.16, bf16[128,4096]{1,0:T(8,128)(2,1)S(1)} %bitcast.18, bf16[128,4096]{1,0:T(8,128)(2,1)S(1)} %bitcast.20), custom_call_target="tpu_custom_call" | custom-call | tf_op jit(solution)/shard_map/products/pallas_call | solution.py:316
Async XLA Ops:
  7.2 1.2 copy-start.1
  8.4 1.2 copy-start.3
  9.6 1.2 copy-start.5
  10.8 1.2 copy-start.11
  14.7 10.5 %copy-start.10 = (bf16[512,256]{1,0:T(8,128)(2,1)S(1)}, bf16[512,256]{1,0:T(8,128)(2,1)}, u32[]{:S(2)}) copy-start(bf16[512,256]{1,0:T(8,128)(2,1)} %constant.17.clone.upper_ref.forward_ref) | copy-start | bytes 786436
  14.7 10.5 %copy-start.13 = (bf16[512,256]{1,0:T(8,128)(2,1)S(1)}, bf16[512,256]{1,0:T(8,128)(2,1)}, u32[]{:S(2)}) copy-start(bf16[512,256]{1,0:T(8,128)(2,1)} %constant.18.clone.lower_ref) | copy-start | bytes 786436
  14.7 39.8 %all-to-all-start = ((bf16[64,2,64,128]{3,2,1,0:T(8,128)(2,1)}), bf16[64,2,64,128]{3,2,1,0:T(8,128)(2,1)S(1)}, u32[]{:S(2)}, u32[]{:S(2)}) async-start(bf16[64,2,64,128]{3,2,1,0:T(8,128)(2,1)} %bitcast.24), calls=%async_computation | async-start | bytes 4194304 | tf_op jit(solution)/shard_map/all_to_all | solution.py:264
  25.3 1.6 %copy-start.7 = (f32[2048,256]{1,0:T(8,128)S(1)}, f32[2048,256]{1,0:T(8,128)}, u32[]{:S(2)}) copy-start(f32[2048,256]{1,0:T(8,128)} %taps_ref.1) | copy-start | bytes 6291460
  26.8 27.7 %copy-start.12 = (bf16[256,512]{1,0:T(8,128)(2,1)S(1)}, bf16[256,512]{1,0:T(8,128)(2,1)}, u32[]{:S(2)}) copy-start(bf16[256,512]{1,0:T(8,128)(2,1)} %constant.19.clone.inverse_ref) | copy-start | bytes 786436
  28.8 1.3 %copy-start = (f32[8,512,128]{2,1,0:T(8,128)}, f32[8,512,128]{2,1,0:T(8,128)S(1)}, u32[]{:S(2)}) copy-start(f32[8,512,128]{2,1,0:T(8,128)S(1)} %filter_spectra.1.filt_ref) | copy-start | bytes 6291460
  68.4 1.3 %copy-start.8 = (bf16[4,16,2,64,128]{4,3,2,1,0:T(8,128)(2,1)}, bf16[4,16,2,64,128]{4,3,2,1,0:T(8,128)(2,1)S(1)}, u32[]{:S(2)}) copy-start(bf16[4,16,2,64,128]{4,3,2,1,0:T(8,128)(2,1)S(1)} %get-tuple-element.9) | copy-start | bytes 6291460
  69.7 10.0 %collective-permute-start = (bf16[1024,128]{1,0:T(8,128)(2,1)S(1)}, bf16[1024,128]{1,0:T(8,128)(2,1)}, u32[]{:S(2)}, u32[]{:S(2)}) collective-permute-start(bf16[1024,128]{1,0:T(8,128)(2,1)S(1)} %get-tuple-element.13), channel_id=1, source_target_pairs={{0,64},{16,80},{32,96},{48,112},{64,0},{80,16},{96,32},{112,48},{1... | collective-permute-start | bytes 786440 | tf_op jit(solution)/shard_map/ppermute | solution.py:302
  73.0 43.4 %all-to-all-start.1 = ((bf16[64,2,64,128]{3,2,1,0:T(8,128)(2,1)}), bf16[64,2,64,128]{3,2,1,0:T(8,128)(2,1)S(1)}, u32[]{:S(2)}, u32[]{:S(2)}) async-start(bf16[64,2,64,128]{3,2,1,0:T(8,128)(2,1)} %bitcast.21), calls=%async_computation.1 | async-start | bytes 4194304 | tf_op jit(solution)/shard_map/all_to_all | solution.py:264
  77.9 38.4 %copy-start.2 = (bf16[1,128,4096]{2,1,0:T(8,128)(2,1)S(1)}, bf16[1,128,4096]{2,1,0:T(8,128)(2,1)}, u32[]{:S(2)}) copy-start(bf16[1,128,4096]{2,1,0:T(8,128)(2,1)} %param.9) | copy-start | bytes 3145732
  78.0 35.2 %all-gather.3.cloned.1.call-start = ((), (), s32[]{:S(2)}) async-start(), calls=%async_computation.2 | async-start | bytes 1310720 | tf_op jit(solution)/shard_map/all_gather | solution.py:307
  113.2 1.2 copy-start.9
  116.4 1.2 copy-start.4
  117.6 1.2 copy-start.6
Sparse Core Ops, SparseCore 0:
  81.6 31.5 all-gather.2
where the time goes:
time: 131 us; the launch traced here: 129 us
  waiting for transfers between devices  58 us (44%)
  Pallas kernels  23.4 us (18%)
  starting transfers between devices  18.8 us (14%)
  between operations  14.1 us (11%)
  local copies, waits for them, and re-layouts  12.8 us (10%)
  other arithmetic  1.72 us (1%)
    all_gather x1, waiting for transfers between devices, local(): lax.all_gather(summed, 'seq', axis=0, tiled=False, axis_index_groups=[[z...  31.8 us
    all_to_all x2, waiting for transfers between devices, exchange(): lax.all_to_all(flat, ('seq', 'ctx'), 0, 0, tiled=True, axis_index_groups=...  24.5 us
    all_to_all x2, starting transfers between devices, exchange(): lax.all_to_all(flat, ('seq', 'ctx'), 0, 0, tiled=True, axis_index_groups=...  15.4 us
    pallas_call x1, Pallas kernels, local(): pl.pallas_call(conv_kernel, in_specs=[whole] * 4, out_specs=[whole] * 2,...  13.8 us
    unnamed x28, local copies, waits for them, and re-layouts  12.8 us
    ppermute x1, starting transfers between devices, local(): lax.ppermute(part_grad, 'seq', [(s, (s + y_count) % seq_count) for s in r...  3.32 us
    pallas_call x1, Pallas kernels, local(): pl.pallas_call(final_kernel, grid=(steps,), in_specs=[packed_spec] + [gat...  3.16 us
    pallas_call x1, Pallas kernels, local(): pl.pallas_call(gate_kernel, grid=(steps,), in_specs=[gate_in] * 4, out_sp...  2.67 us
  transfers between devices with their start and end apart: 4, of which 3 were waited for; matrix products, arithmetic and copies ran while one was open for 1% of the time, Pallas kernels for 3%

commit v1 on v0

v1 whole, which is shorter than its diff:
```python
import functools
import math
import random

import jax
import jax.numpy as jnp
import numpy as np
from jax import lax
from jax.experimental import pallas as pl
from jax.experimental.pallas import tpu as pltpu
from jax.sharding import PartitionSpec as P

BLOCK = 256
HALF = 64
LANES = 128
F32 = jnp.float32
BF16 = jnp.bfloat16
TILE = 16
CHUNKS = 4
VMEM_LIMIT = 30 * 1024 * 1024
SMALL_LIMIT = 12 * 1024 * 1024


def member_order(count):
    order = list(range(count))
    random.Random(58).shuffle(order)
    return order


def dft_tables():
    freq = np.arange(BLOCK)[:, None] * 2 + 1
    time = np.arange(BLOCK)[None, :]
    angle = (freq * time % (4 * BLOCK)) * (2.0 * math.pi / (4 * BLOCK))
    forward = np.concatenate((np.cos(angle), -np.sin(angle)), axis=0).astype(np.float32)
    upper = forward.astype(jnp.bfloat16)
    lower = (forward - upper.astype(np.float32)).astype(jnp.bfloat16)
    inverse = (forward.T / BLOCK).astype(jnp.bfloat16)
    return upper, lower, inverse


def low_lanes(shape):
    return lax.broadcasted_iota(jnp.int32, shape, len(shape) - 1) < HALF


def swap_halves(first, second):
    mask = low_lanes(first.shape)
    return (
        jnp.where(mask, first, pltpu.roll(second, HALF, 1)),
        jnp.where(mask, pltpu.roll(first, HALF, 1), second),
    )


def row_signs(shape):
    row = lax.broadcasted_iota(jnp.int32, shape, 0)
    return (1 - 2 * (row % 2)).astype(F32)


def gate_kernel(
    q_hbm, k_hbm, v_hbm, u_hbm, out_hbm,
    q_ref, k_ref, v_ref, u_ref, out_ref, in_sem, out_sem, *, slots
):
    half_rows = out_ref.shape[3]
    width = q_ref.shape[1] // CHUNKS
    count = width // BLOCK
    sources = ((q_hbm, q_ref), (k_hbm, k_ref), (v_hbm, v_ref), (u_hbm, u_ref))
    loads = [load_chunk(sources, in_sem, chunk, width) for chunk in range(CHUNKS)]
    for row in loads:
        for copy in row:
            copy.start()
    stores = []
    for chunk in range(CHUNKS):
        for copy in loads[chunk]:
            copy.wait()

        for block in range(chunk * count, (chunk + 1) * count):
            for pair in range(2):
                lanes = pl.ds((block * 2 + pair) * LANES, LANES)
                kv = k_ref[:, lanes].astype(F32) * v_ref[:, lanes].astype(F32)
                gg = u_ref[:, lanes].astype(F32) * q_ref[:, lanes].astype(F32)
                for signal, value in enumerate((kv, gg)):
                    parts = swap_halves(value[:half_rows], value[half_rows:])
                    for odd in range(2):
                        out_ref[2 * pair + odd, block, signal] = parts[odd].astype(BF16)
            for y, row in enumerate(slots):
                copy = pltpu.make_async_copy(
                    out_ref.at[y, block], out_hbm.at[row[block]], out_sem.at[row[block]]
                )
                copy.start()
                stores.append(copy)
    for copy in stores:
        copy.wait()


def load_chunk(pairs, sem, chunk, width):
    lanes = pl.ds(chunk * width, width)
    return [
        pltpu.make_async_copy(source.at[:, lanes], target.at[:, lanes], sem.at[which, chunk])
        for which, (source, target) in enumerate(pairs)
    ]


def filter_kernel(place_ref, taps_ref, upper_ref, lower_ref, out_ref):
    blocks = out_ref.shape[1]
    odd = place_ref[0] % 2
    signs = row_signs((BLOCK, LANES))
    mask = low_lanes((BLOCK, LANES))
    before = None
    for block in range(blocks):
        taps = taps_ref[pl.ds(block * BLOCK, BLOCK), :]
        turned = pltpu.roll(taps, HALF, 1)
        taps = jnp.where(jnp.logical_xor(mask, odd == 1), taps, turned)
        high = taps.astype(BF16)
        low = (taps - high.astype(F32)).astype(BF16)
        spec = jnp.dot(upper_ref[...], high, preferred_element_type=F32)
        spec = spec + jnp.dot(upper_ref[...], low, preferred_element_type=F32)
        spec = spec + jnp.dot(lower_ref[...], high, preferred_element_type=F32)
        real, imag = spec[:BLOCK], spec[BLOCK:]
        after = (real, imag)
        if before is not None:
            real, imag = real - signs * before[1], imag + signs * before[0]
        out_ref[0, block] = real
        out_ref[1, block] = imag
        before = after


def spectrum(arrived_ref, forward_ref, sig_ref, spec_ref, slots, signal):
    half_rows = arrived_ref.shape[2]
    per_block = BLOCK // (2 * half_rows)
    for block in range(spec_ref.shape[0]):
        for part in range(per_block):
            for pair in range(2):
                lanes = pl.ds(pair * LANES, LANES)
                first, second = swap_halves(
                    *(
                        arrived_ref[slots[2 * pair + odd][block * per_block + part], signal].astype(F32)
                        for odd in range(2)
                    )
                )
                at = part * 2 * half_rows
                sig_ref[block, pl.ds(at, half_rows), lanes] = first.astype(BF16)
                sig_ref[block, pl.ds(at + half_rows, half_rows), lanes] = second.astype(BF16)
        spec_ref[block] = jnp.dot(forward_ref[...], sig_ref[block], preferred_element_type=F32)


def total(terms):
    out = None
    for term in terms:
        out = term if out is None else out + term
    return out


def side(real, imag):
    return real, imag - real, real + imag


def multiply(pairs):
    first, second, third = (total([h[i] * x[i] for h, x in pairs]) for i in range(3))
    return first - third, first + second


def multiply_conj(pairs):
    first, second, third = (total([h[i] * x[i] for h, x in pairs]) for i in range(3))
    return first + third, first + second


def tile_slices(step):
    row = pl.multiple_of((step // 2) * TILE, TILE)
    lanes = pl.ds(pl.multiple_of((step % 2) * LANES, LANES), LANES)
    return pl.ds(row, TILE), pl.ds(BLOCK + row, TILE), lanes


def read_tiles(spec_ref, where):
    real_rows, imag_rows, lanes = where
    return [
        (spec_ref[b, real_rows, lanes], spec_ref[b, imag_rows, lanes]) for b in range(spec_ref.shape[0])
    ]


def write_tile(prod_ref, where, block, value):
    real_rows, imag_rows, lanes = where
    prod_ref[block, real_rows, lanes] = value[0].astype(BF16)
    prod_ref[block, imag_rows, lanes] = value[1].astype(BF16)


def cross_kernel(
    arrived_ref, forward_ref, inverse_ref, after_ref, terms_ref,
    sig_ref, value_ref, grad_ref, prod_ref, *, slots
):
    blocks = value_ref.shape[0]
    spectrum(arrived_ref, forward_ref, sig_ref, value_ref, slots, 0)
    spectrum(arrived_ref, forward_ref, sig_ref, grad_ref, slots, 1)
    signs = row_signs((TILE, LANES))

    def tile(step, carry):
        where = tile_slices(step)
        value, grad = read_tiles(value_ref, where), read_tiles(grad_ref, where)
        window = [
            (grad[b][0] + signs * grad[b + 1][1], grad[b][1] - signs * grad[b + 1][0])
            for b in range(blocks - 1)
        ] + [grad[-1]]
        left = [(real - imag, real, imag) for real, imag in value]
        right = [side(*x) for x in window]
        for b in range(blocks):
            write_tile(
                prod_ref, where, b, multiply_conj([(left[j], right[b + j]) for j in range(blocks - b)])
            )
        return carry

    lax.fori_loop(0, BLOCK // TILE * 2, tile, 0)

    mask = low_lanes((BLOCK, LANES))
    folded = []
    for block in range(blocks):
        cross = jnp.dot(inverse_ref[...], prod_ref[block], preferred_element_type=F32)
        cross = cross[:, :LANES] + cross[:, LANES:]
        folded.append(cross + pltpu.roll(cross, HALF, 1))
        if block >= blocks // 2:
            at = block - blocks // 2
            terms_ref[pl.ds(at * BLOCK, BLOCK), :] = jnp.where(
                mask, folded[at], folded[block]
            ).astype(BF16)


def conv_kernel(
    arrived_ref, filt_hbm, forward_ref, inverse_ref, after_ref, out_hbm,
    filt_ref, sig_ref, value_ref, grad_ref, conv_ref, back_ref, out_ref, filt_sem, out_sem, *, slots
):
    load = pltpu.make_async_copy(filt_hbm, filt_ref, filt_sem)
    load.start()
    blocks = value_ref.shape[0]
    half_rows = out_ref.shape[2]
    per_block = BLOCK // (2 * half_rows)
    spectrum(arrived_ref, forward_ref, sig_ref, value_ref, slots, 0)
    spectrum(arrived_ref, forward_ref, sig_ref, grad_ref, slots, 1)
    load.wait()

    def tile(step, carry):
        where = tile_slices(step)
        rows = where[0]
        filt = [(filt_ref[0, b, rows, :], filt_ref[1, b, rows, :]) for b in range(blocks)]
        left = [(real + imag, real, imag) for real, imag in filt]
        right = [side(*x) for x in read_tiles(value_ref, where)]
        for b in range(blocks):
            write_tile(conv_ref, where, b, multiply([(left[j], right[b - j]) for j in range(b + 1)]))
        left = [(real - imag, real, imag) for real, imag in filt]
        right = [side(*x) for x in read_tiles(grad_ref, where)]
        for b in range(blocks):
            write_tile(
                back_ref, where, b, multiply_conj([(left[j], right[b + j]) for j in range(blocks - b)])
            )
        return carry

    lax.fori_loop(0, BLOCK // TILE * 2, tile, 0)

    stores = []
    for block in range(blocks):
        for signal, prod_ref in enumerate((conv_ref, back_ref)):
            result = jnp.dot(inverse_ref[...], prod_ref[block], preferred_element_type=F32)
            for part in range(per_block):
                at = part * 2 * half_rows
                for pair in range(2):
                    lanes = slice(pair * LANES, (pair + 1) * LANES)
                    parts = swap_halves(
                        result[at : at + half_rows, lanes],
                        result[at + half_rows : at + 2 * half_rows, lanes],
                    )
                    for odd in range(2):
                        place = slots[2 * pair + odd][block * per_block + part]
                        out_ref[place, signal] = parts[odd].astype(BF16)
        for part in range(per_block):
            for row in slots:
                place = row[block * per_block + part]
                copy = pltpu.make_async_copy(out_ref.at[place], out_hbm.at[place], out_sem.at[place])
                copy.start()
                stores.append(copy)
    for copy in stores:
        copy.wait()


def final_kernel(
    ret_ref, k_ref, v_ref, u_ref, dq_hbm, dk_hbm, dv_hbm, dq_ref, dk_ref, dv_ref, out_sem, *, slots
):
    half_rows = ret_ref.shape[2]
    width = k_ref.shape[1] // CHUNKS
    count = width // BLOCK
    targets = ((dq_ref, dq_hbm), (dk_ref, dk_hbm), (dv_ref, dv_hbm))
    stores = [load_chunk(targets, out_sem, chunk, width) for chunk in range(CHUNKS)]
    for chunk in range(CHUNKS):
        for block in range(chunk * count, (chunk + 1) * count):
            for pair in range(2):
                lanes = pl.ds((block * 2 + pair) * LANES, LANES)
                conv, back = (
                    swap_halves(
                        *(ret_ref[slots[2 * pair + odd][block], signal].astype(F32) for odd in range(2))
                    )
                    for signal in range(2)
                )
                for part in range(2):
                    rows = pl.ds(part * half_rows, half_rows)
                    dq_ref[rows, lanes] = (u_ref[rows, lanes].astype(F32) * conv[part]).astype(BF16)
                    dk_ref[rows, lanes] = (back[part] * v_ref[rows, lanes].astype(F32)).astype(BF16)
                    dv_ref[rows, lanes] = (back[part] * k_ref[rows, lanes].astype(F32)).astype(BF16)
        for copy in stores[chunk]:
            copy.start()
    for row in stores:
        for copy in row:
            copy.wait()


def spread_kernel(place_ref, own_ref, up_ref, down_ref, far_ref, out_ref, held_ref, *, scale):
    count = held_ref.shape[0]
    rows = held_ref.shape[1]
    place = place_ref[0]
    for ref, shift in ((own_ref, 0), (up_ref, 1), (down_ref, 3), (far_ref, 2)):
        held_ref[lax.rem(place + count - shift, count)] = ref[...]
    for pair in range(2):
        lanes = pl.ds(pair * LANES, LANES)
        first, second = swap_halves(
            held_ref[2 * pair].astype(F32) * scale, held_ref[2 * pair + 1].astype(F32) * scale
        )
        out_ref[pl.ds(0, rows), lanes] = first
        out_ref[pl.ds(rows, rows), lanes] = second


def local(queries, keys_in, value_in, upstream, filter_taps, *, ctx_count, seq_count):
    tokens, channels = queries.shape[1], queries.shape[2]
    length = filter_taps.shape[0]
    blocks = length // BLOCK
    y_count = 4
    z_count = seq_count // y_count
    half_rows = tokens // 2
    tokens_in = [a.reshape(tokens, channels) for a in (queries, keys_in, value_in, upstream)]
    params = pltpu.CompilerParams(vmem_limit_bytes=VMEM_LIMIT)
    upper, lower, inverse = (jnp.asarray(t) for t in dft_tables())
    members = y_count * ctx_count
    order = member_order(members)
    groups = [[z * members + m for m in order] for z in range(z_count)]
    place_of = [[order.index(y * ctx_count + c) for c in range(ctx_count)] for y in range(y_count)]
    hbm = pl.BlockSpec(memory_space=pltpu.HBM)
    whole = pl.BlockSpec(memory_space=pltpu.VMEM)
    scalars = pl.BlockSpec(memory_space=pltpu.SMEM)
    token_tile = pltpu.VMEM((tokens, channels), BF16)
    packed_shape = (members, 2, half_rows, LANES)

    packed = pl.pallas_call(
        functools.partial(gate_kernel, slots=place_of),
        in_specs=[hbm] * 4,
        out_specs=hbm,
        out_shape=pltpu.HBM(packed_shape, BF16),
        scratch_shapes=[token_tile] * 4
        + [
            pltpu.VMEM((y_count, ctx_count) + packed_shape[1:], BF16),
            pltpu.SemaphoreType.DMA((4, CHUNKS)),
            pltpu.SemaphoreType.DMA((members,)),
        ],
        compiler_params=params,
        name="gate",
    )(*(pltpu.with_memory_space_constraint(a, pltpu.HBM) for a in tokens_in))

    def exchange(array):
        return lax.all_to_all(array, ("seq", "ctx"), 0, 0, tiled=True, axis_index_groups=groups)

    arrived = exchange(packed)

    place = lax.rem(lax.axis_index("seq"), y_count).astype(jnp.int32).reshape(1)
    filt = pl.pallas_call(
        filter_kernel,
        grid_spec=pltpu.PrefetchScalarGridSpec(
            num_scalar_prefetch=1,
            grid=(1,),
            in_specs=[
                pl.BlockSpec((length, LANES), lambda i, place: (0, place[0] // 2)),
                pl.BlockSpec((2 * BLOCK, BLOCK), lambda i, place: (0, 0)),
                pl.BlockSpec((2 * BLOCK, BLOCK), lambda i, place: (0, 0)),
            ],
            out_specs=pl.BlockSpec((2, blocks, BLOCK, LANES), lambda i, place: (0, 0, 0, 0)),
        ),
        out_shape=pltpu.HBM((2, blocks, BLOCK, LANES), F32),
        compiler_params=params,
        name="filter_spectra",
    )(place, filter_taps, upper, lower)
    filt = pltpu.with_memory_space_constraint(filt, pltpu.HBM)

    signal_tile = pltpu.VMEM((blocks, BLOCK, 2 * LANES), BF16)
    spectrum_tile = pltpu.VMEM((blocks, 2 * BLOCK, 2 * LANES), F32)
    product_tile = pltpu.VMEM((blocks, 2 * BLOCK, 2 * LANES), BF16)
    part_grad = pl.pallas_call(
        functools.partial(cross_kernel, slots=place_of),
        in_specs=[whole] * 3 + [hbm],
        out_specs=whole,
        out_shape=jax.ShapeDtypeStruct((length // 2, LANES), BF16),
        scratch_shapes=[signal_tile, spectrum_tile, spectrum_tile, product_tile],
        compiler_params=params,
        name="filter_terms",
    )(arrived, upper, inverse, filt)

    outgoing = pl.pallas_call(
        functools.partial(conv_kernel, slots=place_of),
        in_specs=[whole, hbm, whole, whole, pl.BlockSpec(memory_space=pl.ANY)],
        out_specs=hbm,
        out_shape=pltpu.HBM(packed_shape, BF16),
        scratch_shapes=[
            pltpu.VMEM(filt.shape, F32),
            signal_tile,
            spectrum_tile,
            spectrum_tile,
            product_tile,
            product_tile,
            pltpu.VMEM(packed_shape, BF16),
            pltpu.SemaphoreType.DMA,
            pltpu.SemaphoreType.DMA((members,)),
        ],
        compiler_params=params,
        name="convolve",
    )(arrived, filt, upper, inverse, part_grad)
    swapped = lax.ppermute(
        part_grad, "seq", [(s, (s + y_count) % seq_count) for s in range(seq_count)]
    )
    summed = (part_grad.astype(F32) + swapped.astype(F32)).astype(BF16)
    outgoing, summed = lax.optimization_barrier((outgoing, summed))
    others = [
        lax.ppermute(
            summed,
            "seq",
            [(s, s // y_count * y_count + (s + shift) % y_count) for s in range(seq_count)],
        )
        for shift in (1, 3, 2)
    ]
    returned = exchange(outgoing)
    query_grad, key_grad, value_grad = pl.pallas_call(
        functools.partial(final_kernel, slots=place_of),
        in_specs=[whole] * 4,
        out_specs=[hbm] * 3,
        out_shape=[pltpu.HBM((tokens, channels), BF16)] * 3,
        scratch_shapes=[token_tile] * 3 + [pltpu.SemaphoreType.DMA((3, CHUNKS))],
        compiler_params=pltpu.CompilerParams(vmem_limit_bytes=SMALL_LIMIT),
        name="products",
    )(returned, *tokens_in[1:])
    query_grad, summed, *others = lax.optimization_barrier((query_grad, summed, *others))
    filter_grad = pl.pallas_call(
        functools.partial(spread_kernel, scale=1.0 / math.sqrt(length * seq_count)),
        in_specs=[scalars] + [whole] * 4,
        out_specs=whole,
        out_shape=jax.ShapeDtypeStruct((length, 2 * LANES), F32),
        scratch_shapes=[pltpu.VMEM((y_count, length // 2, LANES), BF16)],
        compiler_params=params,
        name="spread",
    )(place, summed, *others)

    return (
        query_grad.reshape(queries.shape),
        key_grad.reshape(queries.shape),
        value_grad.reshape(queries.shape),
        filter_grad,
    )


def solution(mesh):
    return jax.shard_map(
        functools.partial(local, ctx_count=mesh.shape["ctx"], seq_count=mesh.shape["seq"]),
        mesh=mesh,
        in_specs=(
            P("seq", "ctx", None),
            P("seq", "ctx", None),
            P("seq", "ctx", None),
            P("seq", "ctx", None),
            P(None, "ctx"),
        ),
        out_specs=(
            P("seq", "ctx", None),
            P("seq", "ctx", None),
            P("seq", "ctx", None),
            P(None, "ctx"),
        ),
        check_vma=False,
    )
```

time: 131 us -> 109 us (0.83); the launches traced: 129 us -> 109 us
  between operations: 14.1 us -> 0.76 us
  waiting for transfers between devices: 58 us -> 49.1 us
  local copies, waits for them, and re-layouts: 12.8 us -> 4.06 us
  starting transfers between devices: 18.8 us -> 25.4 us
  Pallas kernels: 23.4 us -> 29.2 us
  other arithmetic: 1.72 us -> 0.07 us
    all_gather x1 -> x0, waiting for transfers between devices: 31.8 us -> none  [local(): lax.all_gather(summed, 'seq', axis=0, tiled=False, axis_index_groups=[[z...]
    all_to_all x2, waiting for transfers between devices: 24.5 us -> 44.7 us  [exchange(): lax.all_to_all(array, ('seq', 'ctx'), 0, 0, tiled=True, axis_index_groups...]
    unnamed x28 -> x14, local copies, waits for them, and re-layouts: 12.8 us -> 4.06 us
    all_to_all x2, starting transfers between devices: 15.4 us -> 19.9 us  [exchange(): lax.all_to_all(array, ('seq', 'ctx'), 0, 0, tiled=True, axis_index_groups...]
    ppermute x0 -> x3, waiting for transfers between devices: none -> 4.37 us  [local(): lax.ppermute(summed, 'seq', [(s, s // y_count * y_count + (s + shift) % y...]
    pallas_call x3 -> x4, Pallas kernels: 19.6 us -> 22.8 us  [the longest x1 10.9 us: local(): pl.pallas_call(functools.partial(conv_kernel, slots=place_of), in_specs=[...]
    ppermute x0 -> x3, starting transfers between devices: none -> 2.15 us  [local(): lax.ppermute(summed, 'seq', [(s, s // y_count * y_count + (s + shift) % y...]
    ppermute x1, waiting for transfers between devices: 1.7 us -> 0.01 us  [local(): lax.ppermute(part_grad, 'seq', [(s, (s + y_count) % seq_count) for s in r...]
  transfers between devices with their start and end apart: 4 -> 6, of which waited for: 3 -> 4; matrix products, arithmetic and copies ran while one was open for 1% -> 0% of each run, Pallas kernels for 3% -> 15%
where the time goes in v1:
time: 109 us
  waiting for transfers between devices  49.1 us (45%)
  Pallas kernels  29.2 us (27%)
  starting transfers between devices  25.4 us (23%)
  local copies, waits for them, and re-layouts  4.06 us (4%)
    all_to_all x2, waiting for transfers between devices, exchange(): lax.all_to_all(array, ('seq', 'ctx'), 0, 0, tiled=True, axis_index_groups...  44.7 us
    all_to_all x2, starting transfers between devices, exchange(): lax.all_to_all(array, ('seq', 'ctx'), 0, 0, tiled=True, axis_index_groups...  19.9 us
    pallas_call x1, Pallas kernels, local(): pl.pallas_call(functools.partial(conv_kernel, slots=place_of), in_specs=[...  10.9 us
    pallas_call x1, Pallas kernels, local(): pl.pallas_call(functools.partial(cross_kernel, slots=place_of), in_specs=...  5.5 us
    ppermute x3, waiting for transfers between devices, local(): lax.ppermute(summed, 'seq', [(s, s // y_count * y_count + (s + shift) % y...  4.37 us
    unnamed x14, local copies, waits for them, and re-layouts  4.06 us
    pallas_call x1, Pallas kernels, local(): pl.pallas_call(functools.partial(gate_kernel, slots=place_of), in_specs=[...  3.95 us
    ppermute x1, starting transfers between devices, local(): lax.ppermute(part_grad, 'seq', [(s, (s + y_count) % seq_count) for s in r...  3.38 us
  transfers between devices with their start and end apart: 6, of which 4 were waited for; matrix products, arithmetic and copies ran while one was open for 0% of the time, Pallas kernels for 15%

profile of v1, /device:TPU:1, one launch (start us, length us, event | category | flops | bytes accessed | tf_op | source)
XLA Modules:
  0.0 108.5 jit_solution(9837633301291666676)
XLA Ops:
  0.6 4.0 %gate.1 = bf16[64,2,64,128]{3,2,1,0:T(8,128)(2,1)} custom-call(bf16[128,4096]{1,0:T(8,128)(2,1)} %bitcast.14, bf16[128,4096]{1,0:T(8,128)(2,1)} %bitcast.8, bf16[128,4096]{1,0:T(8,128)(2,1)} %bitcast.10, bf16[128,4096]{1,0:T(8,128)(2,1)} %bitcast.12), custom_call_target="tpu_custom_call" | custom-call | tf_op jit(solution)/shard_map/gate/pallas_call | solution.py:345
  4.6 0.0 copy-start.3
  4.6 0.0 copy-start.6
  4.6 11.4 %all-to-all-start = ((bf16[64,2,64,128]{3,2,1,0:T(8,128)(2,1)}), bf16[64,2,64,128]{3,2,1,0:T(8,128)(2,1)S(1)}, u32[]{:S(2)}, u32[]{:S(2)}) async-start(bf16[64,2,64,128]{3,2,1,0:T(8,128)(2,1)} %gate.1), calls=%async_computation | async-start | bytes 4194304 | tf_op jit(solution)/shard_map/all_to_all | solution.py:361
  16.0 0.0 copy-done.3
  16.0 0.0 copy-done.6
  16.1 0.0 copy-start.4
  16.1 1.6 %copy-done.4 = f32[2048,256]{1,0:T(8,128)S(1)} copy-done((f32[2048,256]{1,0:T(8,128)S(1)}, f32[2048,256]{1,0:T(8,128)}, u32[]{:S(2)}) %copy-start.4) | copy-done | bytes 2097176
  17.7 0.0 copy-start.5
  17.7 3.2 %filter_spectra.1.after_ref.filt_hbm = f32[2,8,256,128]{3,2,1,0:T(8,128)} custom-call(s32[1]{0:T(128)} %bitcast.4.place_ref, f32[2048,256]{1,0:T(8,128)S(1)} %copy-done.4, bf16[512,256]{1,0:T(8,128)(2,1)S(1)} %copy-done.3, bf16[512,256]{1,0:T(8,128)(2,1)S(1)} %copy-done.6), custom_call_target="tpu_custom_call" | custom-call | tf_op jit(solution)/shard_map/filter_spectra/pallas_call | solution.py:366
  20.9 20.9 %all-to-all-done.arrived_ref = bf16[64,2,64,128]{3,2,1,0:T(8,128)(2,1)S(1)} async-done(((bf16[64,2,64,128]{3,2,1,0:T(8,128)(2,1)}), bf16[64,2,64,128]{3,2,1,0:T(8,128)(2,1)S(1)}, u32[]{:S(2)}, u32[]{:S(2)}) %all-to-all-start) | async-done | bytes 2097184 | tf_op jit(solution)/shard_map/all_to_all | solution.py:361
  41.8 0.0 copy-done.5
  41.8 5.5 %filter_terms.1.after_ref = bf16[1024,128]{1,0:T(8,128)(2,1)S(1)} custom-call(bf16[64,2,64,128]{3,2,1,0:T(8,128)(2,1)S(1)} %all-to-all-done.arrived_ref, bf16[512,256]{1,0:T(8,128)(2,1)S(1)} %copy-done.3, bf16[256,512]{1,0:T(8,128)(2,1)S(1)} %copy-done.5, f32[2,8,256,128]{3,2,1,0:T(8,128)} %filter_spectra.1.after_ref.filt_hbm), custom_call_target="tpu_custom_call" | custom-call | tf_op jit(solution)/shard_map/filter_terms/pallas_call | solution.py:387
  47.3 3.4 %collective-permute-start = (bf16[1024,128]{1,0:T(8,128)(2,1)S(1)}, bf16[1024,128]{1,0:T(8,128)(2,1)S(1)}, u32[]{:S(2)}, u32[]{:S(2)}) collective-permute-start(bf16[1024,128]{1,0:T(8,128)(2,1)S(1)} %filter_terms.1.after_ref), channel_id=1, source_target_pairs={{0,64},{16,80},{32,96},{48,112},{64,0},{80,16},{96,32},{112,48},{1... | collective-permute-start | bytes 786440 | tf_op jit(solution)/shard_map/ppermute | solution.py:416
  50.7 10.9 %convolve.1 = bf16[64,2,64,128]{3,2,1,0:T(8,128)(2,1)} custom-call(bf16[64,2,64,128]{3,2,1,0:T(8,128)(2,1)S(1)} %all-to-all-done.arrived_ref, f32[2,8,256,128]{3,2,1,0:T(8,128)} %filter_spectra.1.after_ref.filt_hbm, bf16[512,256]{1,0:T(8,128)(2,1)S(1)} %copy-done.3, bf16[256,512]{1,0:T(8,128)(2,1)S(1)} %copy-done.5, bf16[1024,128]{1,0:T(8,128)(2,1)S(1)} %filter_terms.1.after_ref), custom_call_target="tpu_custom_call" | custom-call | tf_op jit(solution)/shard_map/convolve/pallas_call | solution.py:397
  61.7 0.0 collective-permute-done
  61.7 0.1 add_convert_fusion.own_ref
  61.8 0.0 copy-start
  61.8 8.5 %all-to-all-start.1 = ((bf16[64,2,64,128]{3,2,1,0:T(8,128)(2,1)}), bf16[64,2,64,128]{3,2,1,0:T(8,128)(2,1)S(1)}, u32[]{:S(2)}, u32[]{:S(2)}) async-start(bf16[64,2,64,128]{3,2,1,0:T(8,128)(2,1)} %convolve.1), calls=%async_computation.1 | async-start | bytes 4194304 | tf_op jit(solution)/shard_map/all_to_all | solution.py:361
  70.3 0.4 collective-permute-start.3
  70.6 1.8 %collective-permute-start.2 = (bf16[1024,128]{1,0:T(8,128)(2,1)S(1)}, bf16[1024,128]{1,0:T(8,128)(2,1)}, u32[]{:S(2)}, u32[]{:S(2)}) collective-permute-start(bf16[1024,128]{1,0:T(8,128)(2,1)S(1)} %add_convert_fusion.own_ref), channel_id=1, source_target_pairs={{0,48},{16,0},{32,16},{48,32},{64,112},{80,64},{96,80},{112,96},{1... | collective-permute-start | bytes 786440 | tf_op jit(solution)/shard_map/ppermute | solution.py:422
  72.4 0.0 collective-permute-start.1
  72.4 23.8 %all-to-all-done.1.ret_ref = bf16[64,2,64,128]{3,2,1,0:T(8,128)(2,1)S(1)} async-done(((bf16[64,2,64,128]{3,2,1,0:T(8,128)(2,1)}), bf16[64,2,64,128]{3,2,1,0:T(8,128)(2,1)S(1)}, u32[]{:S(2)}, u32[]{:S(2)}) %all-to-all-start.1) | async-done | bytes 2097184 | tf_op jit(solution)/shard_map/all_to_all | solution.py:361
  96.2 0.0 copy-done
  96.2 0.0 copy-start.1
  96.2 1.2 %copy-done.1 = bf16[1,128,4096]{2,1,0:T(8,128)(2,1)S(1)} copy-done((bf16[1,128,4096]{2,1,0:T(8,128)(2,1)S(1)}, bf16[1,128,4096]{2,1,0:T(8,128)(2,1)}, u32[]{:S(2)}) %copy-start.1) | copy-done | bytes 1048600
  97.4 0.0 copy-start.2
  97.4 1.2 %copy-done.2 = bf16[1,128,4096]{2,1,0:T(8,128)(2,1)S(1)} copy-done((bf16[1,128,4096]{2,1,0:T(8,128)(2,1)S(1)}, bf16[1,128,4096]{2,1,0:T(8,128)(2,1)}, u32[]{:S(2)}) %copy-start.2) | copy-done | bytes 1048600
  98.6 2.4 %products.1 = (bf16[128,4096]{1,0:T(8,128)(2,1)}, bf16[128,4096]{1,0:T(8,128)(2,1)}, bf16[128,4096]{1,0:T(8,128)(2,1)}) custom-call(bf16[64,2,64,128]{3,2,1,0:T(8,128)(2,1)S(1)} %all-to-all-done.1.ret_ref, bf16[128,4096]{1,0:T(8,128)(2,1)S(1)} %bitcast.9, bf16[128,4096]{1,0:T(8,128)(2,1)S(1)} %bitcast.11, bf16[128,4096]{1,0:T(8,128)(2,1)S(1)} %bitcast.13), custom_call_target="tpu_custom_call" | custom-call | tf_op jit(solution)/shard_map/products/pallas_call | solution.py:430
  101.0 0.0 collective-permute-done.3.far_ref
  101.0 4.0 %collective-permute-done.2.down_ref = bf16[1024,128]{1,0:T(8,128)(2,1)} collective-permute-done((bf16[1024,128]{1,0:T(8,128)(2,1)S(1)}, bf16[1024,128]{1,0:T(8,128)(2,1)}, u32[]{:S(2)}, u32[]{:S(2)}) %collective-permute-start.2) | collective-permute-done | bytes 262176 | tf_op jit(solution)/shard_map/ppermute | solution.py:422
  105.1 0.3 collective-permute-done.1.up_ref
  105.4 3.1 %spread.1 = f32[2048,256]{1,0:T(8,128)} custom-call(s32[1]{0:T(128)} %bitcast.4.place_ref, bf16[1024,128]{1,0:T(8,128)(2,1)S(1)} %add_convert_fusion.own_ref, bf16[1024,128]{1,0:T(8,128)(2,1)} %collective-permute-done.1.up_ref, bf16[1024,128]{1,0:T(8,128)(2,1)} %collective-permute-done.2.down_ref, bf16[1024,128]{1,0:T(8,128)(2,1)} %collective-permute-done.3.far_ref), custom_call_target="tpu_custom_call" | custom-call | tf_op jit(solution)/shard_map/spread/pallas_call | solution.py:440
Async XLA Ops:
  4.6 11.4 %copy-start.3 = (bf16[512,256]{1,0:T(8,128)(2,1)S(1)}, bf16[512,256]{1,0:T(8,128)(2,1)}, u32[]{:S(2)}) copy-start(bf16[512,256]{1,0:T(8,128)(2,1)} %constant.17.clone.upper_ref.forward_ref) | copy-start | bytes 786436
  4.6 11.4 %copy-start.6 = (bf16[512,256]{1,0:T(8,128)(2,1)S(1)}, bf16[512,256]{1,0:T(8,128)(2,1)}, u32[]{:S(2)}) copy-start(bf16[512,256]{1,0:T(8,128)(2,1)} %constant.18.clone.lower_ref) | copy-start | bytes 786436
  4.6 37.2 %all-to-all-start = ((bf16[64,2,64,128]{3,2,1,0:T(8,128)(2,1)}), bf16[64,2,64,128]{3,2,1,0:T(8,128)(2,1)S(1)}, u32[]{:S(2)}, u32[]{:S(2)}) async-start(bf16[64,2,64,128]{3,2,1,0:T(8,128)(2,1)} %gate.1), calls=%async_computation | async-start | bytes 4194304 | tf_op jit(solution)/shard_map/all_to_all | solution.py:361
  16.1 1.6 %copy-start.4 = (f32[2048,256]{1,0:T(8,128)S(1)}, f32[2048,256]{1,0:T(8,128)}, u32[]{:S(2)}) copy-start(f32[2048,256]{1,0:T(8,128)} %taps_ref.1) | copy-start | bytes 6291460
  17.7 24.2 %copy-start.5 = (bf16[256,512]{1,0:T(8,128)(2,1)S(1)}, bf16[256,512]{1,0:T(8,128)(2,1)}, u32[]{:S(2)}) copy-start(bf16[256,512]{1,0:T(8,128)(2,1)} %constant.19.clone.inverse_ref) | copy-start | bytes 786436
  47.3 14.3 %collective-permute-start = (bf16[1024,128]{1,0:T(8,128)(2,1)S(1)}, bf16[1024,128]{1,0:T(8,128)(2,1)S(1)}, u32[]{:S(2)}, u32[]{:S(2)}) collective-permute-start(bf16[1024,128]{1,0:T(8,128)(2,1)S(1)} %filter_terms.1.after_ref), channel_id=1, source_target_pairs={{0,64},{16,80},{32,96},{48,112},{64,0},{80,16},{96,32},{112,48},{1... | collective-permute-start | bytes 786440 | tf_op jit(solution)/shard_map/ppermute | solution.py:416
  61.8 34.4 %copy-start = (bf16[1,128,4096]{2,1,0:T(8,128)(2,1)S(1)}, bf16[1,128,4096]{2,1,0:T(8,128)(2,1)}, u32[]{:S(2)}) copy-start(bf16[1,128,4096]{2,1,0:T(8,128)(2,1)} %param.9) | copy-start | bytes 3145732
  61.8 34.4 %all-to-all-start.1 = ((bf16[64,2,64,128]{3,2,1,0:T(8,128)(2,1)}), bf16[64,2,64,128]{3,2,1,0:T(8,128)(2,1)S(1)}, u32[]{:S(2)}, u32[]{:S(2)}) async-start(bf16[64,2,64,128]{3,2,1,0:T(8,128)(2,1)} %convolve.1), calls=%async_computation.1 | async-start | bytes 4194304 | tf_op jit(solution)/shard_map/all_to_all | solution.py:361
  70.3 30.8 %collective-permute-start.3 = (bf16[1024,128]{1,0:T(8,128)(2,1)S(1)}, bf16[1024,128]{1,0:T(8,128)(2,1)}, u32[]{:S(2)}, u32[]{:S(2)}) collective-permute-start(bf16[1024,128]{1,0:T(8,128)(2,1)S(1)} %add_convert_fusion.own_ref), channel_id=1, source_target_pairs={{0,32},{16,48},{32,0},{48,16},{64,96},{80,112},{96,64},{112,80},{1... | collective-permute-start | bytes 786440 | tf_op jit(solution)/shard_map/ppermute | solution.py:422
  70.6 34.4 %collective-permute-start.2 = (bf16[1024,128]{1,0:T(8,128)(2,1)S(1)}, bf16[1024,128]{1,0:T(8,128)(2,1)}, u32[]{:S(2)}, u32[]{:S(2)}) collective-permute-start(bf16[1024,128]{1,0:T(8,128)(2,1)S(1)} %add_convert_fusion.own_ref), channel_id=1, source_target_pairs={{0,48},{16,0},{32,16},{48,32},{64,112},{80,64},{96,80},{112,96},{1... | collective-permute-start | bytes 786440 | tf_op jit(solution)/shard_map/ppermute | solution.py:422
  72.4 33.0 %collective-permute-start.1 = (bf16[1024,128]{1,0:T(8,128)(2,1)S(1)}, bf16[1024,128]{1,0:T(8,128)(2,1)}, u32[]{:S(2)}, u32[]{:S(2)}) collective-permute-start(bf16[1024,128]{1,0:T(8,128)(2,1)S(1)} %add_convert_fusion.own_ref), channel_id=1, source_target_pairs={{0,16},{16,32},{32,48},{48,0},{64,80},{80,96},{96,112},{112,64},{1... | collective-permute-start | bytes 786440 | tf_op jit(solution)/shard_map/ppermute | solution.py:422
  96.2 1.2 %copy-start.1 = (bf16[1,128,4096]{2,1,0:T(8,128)(2,1)S(1)}, bf16[1,128,4096]{2,1,0:T(8,128)(2,1)}, u32[]{:S(2)}) copy-start(bf16[1,128,4096]{2,1,0:T(8,128)(2,1)} %param.10) | copy-start | bytes 3145732
  97.4 1.2 %copy-start.2 = (bf16[1,128,4096]{2,1,0:T(8,128)(2,1)S(1)}, bf16[1,128,4096]{2,1,0:T(8,128)(2,1)}, u32[]{:S(2)}) copy-start(bf16[1,128,4096]{2,1,0:T(8,128)(2,1)} %param.11) | copy-start | bytes 3145732

commit v2 on v1

--- a/solution.py
+++ b/solution.py
@@ -17,7 +17,7 @@
 BF16 = jnp.bfloat16
 TILE = 16
 CHUNKS = 4
-VMEM_LIMIT = 30 * 1024 * 1024
+VMEM_LIMIT = 24 * 1024 * 1024
 SMALL_LIMIT = 12 * 1024 * 1024
 
 
@@ -183,10 +183,11 @@
 
 
 def cross_kernel(
-    arrived_ref, forward_ref, inverse_ref, after_ref, terms_ref,
-    sig_ref, value_ref, grad_ref, prod_ref, *, slots
+    arrived_ref, forward_ref, inverse_ref, filt_hbm, terms_ref, value_ref, grad_ref, filt_ref,
+    sig_ref, prod_ref, filt_sem, *, slots
 ):
     blocks = value_ref.shape[0]
+    loads = filter_loads(filt_hbm, filt_ref, filt_sem)
     spectrum(arrived_ref, forward_ref, sig_ref, value_ref, slots, 0)
     spectrum(arrived_ref, forward_ref, sig_ref, grad_ref, slots, 1)
     signs = row_signs((TILE, LANES))
@@ -219,20 +220,44 @@
             terms_ref[pl.ds(at * BLOCK, BLOCK), :] = jnp.where(
                 mask, folded[at], folded[block]
             ).astype(BF16)
-
-
-def conv_kernel(
-    arrived_ref, filt_hbm, forward_ref, inverse_ref, after_ref, out_hbm,
-    filt_ref, sig_ref, value_ref, grad_ref, conv_ref, back_ref, out_ref, filt_sem, out_sem, *, slots
-):
-    load = pltpu.make_async_copy(filt_hbm, filt_ref, filt_sem)
-    load.start()
-    blocks = value_ref.shape[0]
+    for copy in loads:
+        copy.wait()
+
+
+def filter_loads(filt_hbm, filt_ref, sem):
+    copies = [
+        pltpu.make_async_copy(filt_hbm.at[kind, block], filt_ref.at[kind, block], sem.at[kind, block])
+        for block in range(filt_ref.shape[1])
+        for kind in range(2)
+    ]
+    for copy in copies:
+        copy.start()
+    return copies
+
+
+def invert_block(inverse_ref, prod_ref, out_ref, block, slots, signal):
     half_rows = out_ref.shape[2]
     per_block = BLOCK // (2 * half_rows)
-    spectrum(arrived_ref, forward_ref, sig_ref, value_ref, slots, 0)
-    spectrum(arrived_ref, forward_ref, sig_ref, grad_ref, slots, 1)
-    load.wait()
+    result = jnp.dot(inverse_ref[...], prod_ref[block], preferred_element_type=F32)
+    places = []
+    for part in range(per_block):
+        at = part * 2 * half_rows
+        for pair in range(2):
+            lanes = slice(pair * LANES, (pair + 1) * LANES)
+            parts = swap_halves(
+                result[at : at + half_rows, lanes], result[at + half_rows : at + 2 * half_rows, lanes]
+            )
+            for odd in range(2):
+                place = slots[2 * pair + odd][block * per_block + part]
+                out_ref[place, signal] = parts[odd].astype(BF16)
+                places.append(place)
+    return places
+
+
+def conv_kernel(
+    value_ref, grad_ref, filt_ref, inverse_ref, out_hbm, conv_ref, back_ref, out_ref, out_sem, *, slots
+):
+    blocks = value_ref.shape[0]
 
     def tile(step, carry):
         where = tile_slices(step)
@@ -251,28 +276,14 @@
         return carry
 
     lax.fori_loop(0, BLOCK // TILE * 2, tile, 0)
-
     stores = []
     for block in range(blocks):
         for signal, prod_ref in enumerate((conv_ref, back_ref)):
-            result = jnp.dot(inverse_ref[...], prod_ref[block], preferred_element_type=F32)
-            for part in range(per_block):
-                at = part * 2 * half_rows
-                for pair in range(2):
-                    lanes = slice(pair * LANES, (pair + 1) * LANES)
-                    parts = swap_halves(
-                        result[at : at + half_rows, lanes],
-                        result[at + half_rows : at + 2 * half_rows, lanes],
-                    )
-                    for odd in range(2):
-                        place = slots[2 * pair + odd][block * per_block + part]
-                        out_ref[place, signal] = parts[odd].astype(BF16)
-        for part in range(per_block):
-            for row in slots:
-                place = row[block * per_block + part]
-                copy = pltpu.make_async_copy(out_ref.at[place], out_hbm.at[place], out_sem.at[place])
-                copy.start()
-                stores.append(copy)
+            places = invert_block(inverse_ref, prod_ref, out_ref, block, slots, signal)
+        for place in places:
+            copy = pltpu.make_async_copy(out_ref.at[place], out_hbm.at[place], out_sem.at[place])
+            copy.start()
+            stores.append(copy)
     for copy in stores:
         copy.wait()
 
@@ -307,19 +318,34 @@
             copy.wait()
 
 
-def spread_kernel(place_ref, own_ref, up_ref, down_ref, far_ref, out_ref, held_ref, *, scale):
+def spread_kernel(
+    place_ref, own_ref, up_ref, down_ref, far_ref, after_ref,
+    out_hbm, held_ref, out_ref, out_sem, *, scale
+):
     count = held_ref.shape[0]
     rows = held_ref.shape[1]
+    step = rows // CHUNKS
     place = place_ref[0]
     for ref, shift in ((own_ref, 0), (up_ref, 1), (down_ref, 3), (far_ref, 2)):
         held_ref[lax.rem(place + count - shift, count)] = ref[...]
-    for pair in range(2):
-        lanes = pl.ds(pair * LANES, LANES)
-        first, second = swap_halves(
-            held_ref[2 * pair].astype(F32) * scale, held_ref[2 * pair + 1].astype(F32) * scale
-        )
-        out_ref[pl.ds(0, rows), lanes] = first
-        out_ref[pl.ds(rows, rows), lanes] = second
+    stores = []
+    for chunk in range(CHUNKS):
+        part = pl.ds(chunk * step, step)
+        for pair in range(2):
+            lanes = pl.ds(pair * LANES, LANES)
+            values = swap_halves(
+                held_ref[2 * pair, part].astype(F32) * scale,
+                held_ref[2 * pair + 1, part].astype(F32) * scale,
+            )
+            for half in range(2):
+                out_ref[pl.ds(half * rows + chunk * step, step), lanes] = values[half]
+        for half in range(2):
+            part = pl.ds(half * rows + chunk * step, step)
+            copy = pltpu.make_async_copy(out_ref.at[part], out_hbm.at[part], out_sem.at[half, chunk])
+            copy.start()
+            stores.append(copy)
+    for copy in stores:
+        copy.wait()
 
 
 def local(queries, keys_in, value_in, upstream, filter_taps, *, ctx_count, seq_count):
@@ -382,37 +408,36 @@
     filt = pltpu.with_memory_space_constraint(filt, pltpu.HBM)
 
     signal_tile = pltpu.VMEM((blocks, BLOCK, 2 * LANES), BF16)
-    spectrum_tile = pltpu.VMEM((blocks, 2 * BLOCK, 2 * LANES), F32)
     product_tile = pltpu.VMEM((blocks, 2 * BLOCK, 2 * LANES), BF16)
-    part_grad = pl.pallas_call(
+    spectrum_shape = jax.ShapeDtypeStruct((blocks, 2 * BLOCK, 2 * LANES), F32)
+    part_grad, value_spec, grad_spec, filt = pl.pallas_call(
         functools.partial(cross_kernel, slots=place_of),
         in_specs=[whole] * 3 + [hbm],
-        out_specs=whole,
-        out_shape=jax.ShapeDtypeStruct((length // 2, LANES), BF16),
-        scratch_shapes=[signal_tile, spectrum_tile, spectrum_tile, product_tile],
+        out_specs=[whole] * 4,
+        out_shape=[
+            jax.ShapeDtypeStruct((length // 2, LANES), BF16),
+            spectrum_shape,
+            spectrum_shape,
+            jax.ShapeDtypeStruct(filt.shape, F32),
+        ],
+        scratch_shapes=[signal_tile, product_tile, pltpu.SemaphoreType.DMA((2, blocks))],
         compiler_params=params,
         name="filter_terms",
     )(arrived, upper, inverse, filt)
-
     outgoing = pl.pallas_call(
         functools.partial(conv_kernel, slots=place_of),
-        in_specs=[whole, hbm, whole, whole, pl.BlockSpec(memory_space=pl.ANY)],
+        in_specs=[whole] * 4,
         out_specs=hbm,
         out_shape=pltpu.HBM(packed_shape, BF16),
         scratch_shapes=[
-            pltpu.VMEM(filt.shape, F32),
-            signal_tile,
-            spectrum_tile,
-            spectrum_tile,
             product_tile,
             product_tile,
             pltpu.VMEM(packed_shape, BF16),
-            pltpu.SemaphoreType.DMA,
             pltpu.SemaphoreType.DMA((members,)),
         ],
         compiler_params=params,
         name="convolve",
-    )(arrived, filt, upper, inverse, part_grad)
+    )(value_spec, grad_spec, filt, inverse)
     swapped = lax.ppermute(
         part_grad, "seq", [(s, (s + y_count) % seq_count) for s in range(seq_count)]
     )
@@ -436,17 +461,19 @@
         compiler_params=pltpu.CompilerParams(vmem_limit_bytes=SMALL_LIMIT),
         name="products",
     )(returned, *tokens_in[1:])
-    query_grad, summed, *others = lax.optimization_barrier((query_grad, summed, *others))
     filter_grad = pl.pallas_call(
         functools.partial(spread_kernel, scale=1.0 / math.sqrt(length * seq_count)),
-        in_specs=[scalars] + [whole] * 4,
-        out_specs=whole,
-        out_shape=jax.ShapeDtypeStruct((length, 2 * LANES), F32),
-        scratch_shapes=[pltpu.VMEM((y_count, length // 2, LANES), BF16)],
-        compiler_params=params,
+        in_specs=[scalars] + [whole] * 4 + [hbm],
+        out_specs=hbm,
+        out_shape=pltpu.HBM((length, 2 * LANES), F32),
+        scratch_shapes=[
+            pltpu.VMEM((y_count, length // 2, LANES), BF16),
+            pltpu.VMEM((length, 2 * LANES), F32),
+            pltpu.SemaphoreType.DMA((2, CHUNKS)),
+        ],
+        compiler_params=pltpu.CompilerParams(vmem_limit_bytes=SMALL_LIMIT),
         name="spread",
-    )(place, summed, *others)
-
+    )(place, summed, *others, pltpu.with_memory_space_constraint(query_grad, pltpu.HBM))
     return (
         query_grad.reshape(queries.shape),
         key_grad.reshape(queries.shape),

time: 109 us -> 106 us (0.972)
  Pallas kernels: 29.2 us -> 25.9 us
    pallas_call x1, Pallas kernels: 10.9 us -> 7.95 us  [local(): pl.pallas_call(functools.partial(conv_kernel, slots=place_of), in_specs=[...]
  transfers between devices with their start and end apart: 6 -> 6, of which waited for: 4 -> 4; matrix products, arithmetic and copies ran while one was open for 0% -> 0% of each run, Pallas kernels for 15% -> 13%
where the time goes in v2:
time: 106 us; the launch traced here: 105 us
  waiting for transfers between devices  49.1 us (46%)
  Pallas kernels  25.9 us (24%)
  starting transfers between devices  25.4 us (24%)
  local copies, waits for them, and re-layouts  4.06 us (4%)
    all_to_all x2, waiting for transfers between devices, exchange(): lax.all_to_all(array, ('seq', 'ctx'), 0, 0, tiled=True, axis_index_groups...  44.7 us
    all_to_all x2, starting transfers between devices, exchange(): lax.all_to_all(array, ('seq', 'ctx'), 0, 0, tiled=True, axis_index_groups...  19.9 us
    pallas_call x1, Pallas kernels, local(): pl.pallas_call(functools.partial(conv_kernel, slots=place_of), in_specs=[...  7.95 us
    pallas_call x1, Pallas kernels, local(): pl.pallas_call(functools.partial(cross_kernel, slots=place_of), in_specs=...  5.62 us
    ppermute x3, waiting for transfers between devices, local(): lax.ppermute(summed, 'seq', [(s, s // y_count * y_count + (s + shift) % y...  4.37 us
    unnamed x14, local copies, waits for them, and re-layouts  4.06 us
    pallas_call x1, Pallas kernels, local(): pl.pallas_call(functools.partial(gate_kernel, slots=place_of), in_specs=[...  3.95 us
    ppermute x1, starting transfers between devices, local(): lax.ppermute(part_grad, 'seq', [(s, (s + y_count) % seq_count) for s in r...  3.38 us
  transfers between devices with their start and end apart: 6, of which 4 were waited for; matrix products, arithmetic and copies ran while one was open for 0% of the time, Pallas kernels for 13%

profile of v2, /device:TPU:1, one launch (start us, length us, event | category | flops | bytes accessed | tf_op | source)
XLA Modules:
  0.0 105.3 jit_solution(7831766154314759901)
XLA Ops:
  0.6 4.0 %gate.1 = bf16[64,2,64,128]{3,2,1,0:T(8,128)(2,1)} custom-call(bf16[128,4096]{1,0:T(8,128)(2,1)} %bitcast.15, bf16[128,4096]{1,0:T(8,128)(2,1)} %bitcast.8, bf16[128,4096]{1,0:T(8,128)(2,1)} %bitcast.10, bf16[128,4096]{1,0:T(8,128)(2,1)} %bitcast.12), custom_call_target="tpu_custom_call" | custom-call | tf_op jit(solution)/shard_map/gate/pallas_call | solution.py:371
  4.6 0.0 copy-start.5
  4.6 0.0 copy-start.6
  4.6 11.4 %all-to-all-start = ((bf16[64,2,64,128]{3,2,1,0:T(8,128)(2,1)}), bf16[64,2,64,128]{3,2,1,0:T(8,128)(2,1)S(1)}, u32[]{:S(2)}, u32[]{:S(2)}) async-start(bf16[64,2,64,128]{3,2,1,0:T(8,128)(2,1)} %gate.1), calls=%async_computation | async-start | bytes 4194304 | tf_op jit(solution)/shard_map/all_to_all | solution.py:387
  16.0 0.0 copy-done.5
  16.0 0.0 copy-done.6
  16.1 0.0 copy-start.3
  16.1 1.6 %copy-done.3 = f32[2048,256]{1,0:T(8,128)S(1)} copy-done((f32[2048,256]{1,0:T(8,128)S(1)}, f32[2048,256]{1,0:T(8,128)}, u32[]{:S(2)}) %copy-start.3) | copy-done | bytes 2097176
  17.7 0.0 copy-start.4
  17.7 3.2 %filter_spectra.1.filt_hbm = f32[2,8,256,128]{3,2,1,0:T(8,128)} custom-call(s32[1]{0:T(128)} %bitcast.4.place_ref, f32[2048,256]{1,0:T(8,128)S(1)} %copy-done.3, bf16[512,256]{1,0:T(8,128)(2,1)S(1)} %copy-done.5, bf16[512,256]{1,0:T(8,128)(2,1)S(1)} %copy-done.6), custom_call_target="tpu_custom_call" | custom-call | tf_op jit(solution)/shard_map/filter_spectra/pallas_call | solution.py:392
  20.9 20.9 %all-to-all-done.arrived_ref = bf16[64,2,64,128]{3,2,1,0:T(8,128)(2,1)S(1)} async-done(((bf16[64,2,64,128]{3,2,1,0:T(8,128)(2,1)}), bf16[64,2,64,128]{3,2,1,0:T(8,128)(2,1)S(1)}, u32[]{:S(2)}, u32[]{:S(2)}) %all-to-all-start) | async-done | bytes 2097184 | tf_op jit(solution)/shard_map/all_to_all | solution.py:387
  41.8 0.0 copy-done.4
  41.8 5.6 %filter_terms.1 = (bf16[1024,128]{1,0:T(8,128)(2,1)S(1)}, f32[8,512,256]{2,1,0:T(8,128)S(1)}, f32[8,512,256]{2,1,0:T(8,128)S(1)}, f32[2,8,256,128]{3,2,1,0:T(8,128)S(1)}) custom-call(bf16[64,2,64,128]{3,2,1,0:T(8,128)(2,1)S(1)} %all-to-all-done.arrived_ref, bf16[512,256]{1,0:T(8,128)(2,1)S(1)} %copy-done.5, bf16[256,512]{1,0:T(8,128)(2,1)S(1)} %copy-done.4, ...), custom_call_target="tpu_custom_call" | custom-call | tf_op jit(solution)/shard_map/filter_terms/pallas_call | solution.py:413
  47.5 3.4 %collective-permute-start = (bf16[1024,128]{1,0:T(8,128)(2,1)S(1)}, bf16[1024,128]{1,0:T(8,128)(2,1)S(1)}, u32[]{:S(2)}, u32[]{:S(2)}) collective-permute-start(bf16[1024,128]{1,0:T(8,128)(2,1)S(1)} %get-tuple-element.16), channel_id=1, source_target_pairs={{0,64},{16,80},{32,96},{48,112},{64,0},{80,16},{96,32},{112,48},{1... | collective-permute-start | bytes 786440 | tf_op jit(solution)/shard_map/ppermute | solution.py:441
  50.8 8.0 %convolve.1 = bf16[64,2,64,128]{3,2,1,0:T(8,128)(2,1)} custom-call(f32[8,512,256]{2,1,0:T(8,128)S(1)} %get-tuple-element.13.value_ref, f32[8,512,256]{2,1,0:T(8,128)S(1)} %get-tuple-element.14.grad_ref, f32[2,8,256,128]{3,2,1,0:T(8,128)S(1)} %get-tuple-element.15.filt_ref, bf16[256,512]{1,0:T(8,128)(2,1)S(1)} %copy-done.4), custom_call_target="tpu_custom_call" | custom-call | tf_op jit(solution)/shard_map/convolve/pallas_call | solution.py:427
  58.8 0.0 collective-permute-done
  58.8 0.1 add_convert_fusion.own_ref
  58.9 0.0 copy-start
  58.9 8.5 %all-to-all-start.1 = ((bf16[64,2,64,128]{3,2,1,0:T(8,128)(2,1)}), bf16[64,2,64,128]{3,2,1,0:T(8,128)(2,1)S(1)}, u32[]{:S(2)}, u32[]{:S(2)}) async-start(bf16[64,2,64,128]{3,2,1,0:T(8,128)(2,1)} %convolve.1), calls=%async_computation.1 | async-start | bytes 4194304 | tf_op jit(solution)/shard_map/all_to_all | solution.py:387
  67.4 0.4 collective-permute-start.3
  67.8 1.8 %collective-permute-start.2 = (bf16[1024,128]{1,0:T(8,128)(2,1)S(1)}, bf16[1024,128]{1,0:T(8,128)(2,1)}, u32[]{:S(2)}, u32[]{:S(2)}) collective-permute-start(bf16[1024,128]{1,0:T(8,128)(2,1)S(1)} %add_convert_fusion.own_ref), channel_id=1, source_target_pairs={{0,48},{16,0},{32,16},{48,32},{64,112},{80,64},{96,80},{112,96},{1... | collective-permute-start | bytes 786440 | tf_op jit(solution)/shard_map/ppermute | solution.py:447
  69.5 0.0 collective-permute-start.1
  69.5 23.8 %all-to-all-done.1.ret_ref = bf16[64,2,64,128]{3,2,1,0:T(8,128)(2,1)S(1)} async-done(((bf16[64,2,64,128]{3,2,1,0:T(8,128)(2,1)}), bf16[64,2,64,128]{3,2,1,0:T(8,128)(2,1)S(1)}, u32[]{:S(2)}, u32[]{:S(2)}) %all-to-all-start.1) | async-done | bytes 2097184 | tf_op jit(solution)/shard_map/all_to_all | solution.py:387
  93.3 0.0 copy-done
  93.3 0.0 copy-start.1
  93.3 1.2 %copy-done.1 = bf16[1,128,4096]{2,1,0:T(8,128)(2,1)S(1)} copy-done((bf16[1,128,4096]{2,1,0:T(8,128)(2,1)S(1)}, bf16[1,128,4096]{2,1,0:T(8,128)(2,1)}, u32[]{:S(2)}) %copy-start.1) | copy-done | bytes 1048600
  94.5 0.0 copy-start.2
  94.5 1.2 %copy-done.2 = bf16[1,128,4096]{2,1,0:T(8,128)(2,1)S(1)} copy-done((bf16[1,128,4096]{2,1,0:T(8,128)(2,1)S(1)}, bf16[1,128,4096]{2,1,0:T(8,128)(2,1)}, u32[]{:S(2)}) %copy-start.2) | copy-done | bytes 1048600
  95.8 2.4 %products.1 = (bf16[128,4096]{1,0:T(8,128)(2,1)}, bf16[128,4096]{1,0:T(8,128)(2,1)}, bf16[128,4096]{1,0:T(8,128)(2,1)}) custom-call(bf16[64,2,64,128]{3,2,1,0:T(8,128)(2,1)S(1)} %all-to-all-done.1.ret_ref, bf16[128,4096]{1,0:T(8,128)(2,1)S(1)} %bitcast.9, bf16[128,4096]{1,0:T(8,128)(2,1)S(1)} %bitcast.11, bf16[128,4096]{1,0:T(8,128)(2,1)S(1)} %bitcast.13), custom_call_target="tpu_custom_call" | custom-call | tf_op jit(solution)/shard_map/products/pallas_call | solution.py:455
  98.1 0.0 collective-permute-done.3.far_ref
  98.2 4.0 %collective-permute-done.2.down_ref = bf16[1024,128]{1,0:T(8,128)(2,1)} collective-permute-done((bf16[1024,128]{1,0:T(8,128)(2,1)S(1)}, bf16[1024,128]{1,0:T(8,128)(2,1)}, u32[]{:S(2)}, u32[]{:S(2)}) %collective-permute-start.2) | collective-permute-done | bytes 262176 | tf_op jit(solution)/shard_map/ppermute | solution.py:447
  102.2 0.3 collective-permute-done.1.up_ref
  102.5 2.8 %spread.1 = f32[2048,256]{1,0:T(8,128)} custom-call(s32[1]{0:T(128)} %bitcast.4.place_ref, bf16[1024,128]{1,0:T(8,128)(2,1)S(1)} %add_convert_fusion.own_ref, bf16[1024,128]{1,0:T(8,128)(2,1)} %collective-permute-done.1.up_ref, bf16[1024,128]{1,0:T(8,128)(2,1)} %collective-permute-done.2.down_ref, bf16[1024,128]{1,0:T(8,128)(2,1)} %collective-permute-done.3.far_ref, ...), custom_call_target="tpu_custom_call" | custom-call | tf_op jit(solution)/shard_map/spread/pallas_call | solution.py:464
Async XLA Ops:
  4.6 11.4 %copy-start.5 = (bf16[512,256]{1,0:T(8,128)(2,1)S(1)}, bf16[512,256]{1,0:T(8,128)(2,1)}, u32[]{:S(2)}) copy-start(bf16[512,256]{1,0:T(8,128)(2,1)} %constant.17.clone.upper_ref.forward_ref) | copy-start | bytes 786436
  4.6 11.4 %copy-start.6 = (bf16[512,256]{1,0:T(8,128)(2,1)S(1)}, bf16[512,256]{1,0:T(8,128)(2,1)}, u32[]{:S(2)}) copy-start(bf16[512,256]{1,0:T(8,128)(2,1)} %constant.18.clone.lower_ref) | copy-start | bytes 786436
  4.6 37.2 %all-to-all-start = ((bf16[64,2,64,128]{3,2,1,0:T(8,128)(2,1)}), bf16[64,2,64,128]{3,2,1,0:T(8,128)(2,1)S(1)}, u32[]{:S(2)}, u32[]{:S(2)}) async-start(bf16[64,2,64,128]{3,2,1,0:T(8,128)(2,1)} %gate.1), calls=%async_computation | async-start | bytes 4194304 | tf_op jit(solution)/shard_map/all_to_all | solution.py:387
  16.1 1.6 %copy-start.3 = (f32[2048,256]{1,0:T(8,128)S(1)}, f32[2048,256]{1,0:T(8,128)}, u32[]{:S(2)}) copy-start(f32[2048,256]{1,0:T(8,128)} %taps_ref.1) | copy-start | bytes 6291460
  17.7 24.2 %copy-start.4 = (bf16[256,512]{1,0:T(8,128)(2,1)S(1)}, bf16[256,512]{1,0:T(8,128)(2,1)}, u32[]{:S(2)}) copy-start(bf16[256,512]{1,0:T(8,128)(2,1)} %constant.19.clone.inverse_ref) | copy-start | bytes 786436
  47.5 11.3 %collective-permute-start = (bf16[1024,128]{1,0:T(8,128)(2,1)S(1)}, bf16[1024,128]{1,0:T(8,128)(2,1)S(1)}, u32[]{:S(2)}, u32[]{:S(2)}) collective-permute-start(bf16[1024,128]{1,0:T(8,128)(2,1)S(1)} %get-tuple-element.16), channel_id=1, source_target_pairs={{0,64},{16,80},{32,96},{48,112},{64,0},{80,16},{96,32},{112,48},{1... | collective-permute-start | bytes 786440 | tf_op jit(solution)/shard_map/ppermute | solution.py:441
  58.9 34.4 %copy-start = (bf16[1,128,4096]{2,1,0:T(8,128)(2,1)S(1)}, bf16[1,128,4096]{2,1,0:T(8,128)(2,1)}, u32[]{:S(2)}) copy-start(bf16[1,128,4096]{2,1,0:T(8,128)(2,1)} %param.9) | copy-start | bytes 3145732
  58.9 34.4 %all-to-all-start.1 = ((bf16[64,2,64,128]{3,2,1,0:T(8,128)(2,1)}), bf16[64,2,64,128]{3,2,1,0:T(8,128)(2,1)S(1)}, u32[]{:S(2)}, u32[]{:S(2)}) async-start(bf16[64,2,64,128]{3,2,1,0:T(8,128)(2,1)} %convolve.1), calls=%async_computation.1 | async-start | bytes 4194304 | tf_op jit(solution)/shard_map/all_to_all | solution.py:387
  67.4 30.8 %collective-permute-start.3 = (bf16[1024,128]{1,0:T(8,128)(2,1)S(1)}, bf16[1024,128]{1,0:T(8,128)(2,1)}, u32[]{:S(2)}, u32[]{:S(2)}) collective-permute-start(bf16[1024,128]{1,0:T(8,128)(2,1)S(1)} %add_convert_fusion.own_ref), channel_id=1, source_target_pairs={{0,32},{16,48},{32,0},{48,16},{64,96},{80,112},{96,64},{112,80},{1... | collective-permute-start | bytes 786440 | tf_op jit(solution)/shard_map/ppermute | solution.py:447
  67.8 34.4 %collective-permute-start.2 = (bf16[1024,128]{1,0:T(8,128)(2,1)S(1)}, bf16[1024,128]{1,0:T(8,128)(2,1)}, u32[]{:S(2)}, u32[]{:S(2)}) collective-permute-start(bf16[1024,128]{1,0:T(8,128)(2,1)S(1)} %add_convert_fusion.own_ref), channel_id=1, source_target_pairs={{0,48},{16,0},{32,16},{48,32},{64,112},{80,64},{96,80},{112,96},{1... | collective-permute-start | bytes 786440 | tf_op jit(solution)/shard_map/ppermute | solution.py:447
  69.5 33.0 %collective-permute-start.1 = (bf16[1024,128]{1,0:T(8,128)(2,1)S(1)}, bf16[1024,128]{1,0:T(8,128)(2,1)}, u32[]{:S(2)}, u32[]{:S(2)}) collective-permute-start(bf16[1024,128]{1,0:T(8,128)(2,1)S(1)} %add_convert_fusion.own_ref), channel_id=1, source_target_pairs={{0,16},{16,32},{32,48},{48,0},{64,80},{80,96},{96,112},{112,64},{1... | collective-permute-start | bytes 786440 | tf_op jit(solution)/shard_map/ppermute | solution.py:447
  93.3 1.2 %copy-start.1 = (bf16[1,128,4096]{2,1,0:T(8,128)(2,1)S(1)}, bf16[1,128,4096]{2,1,0:T(8,128)(2,1)}, u32[]{:S(2)}) copy-start(bf16[1,128,4096]{2,1,0:T(8,128)(2,1)} %param.10) | copy-start | bytes 3145732
  94.5 1.2 %copy-start.2 = (bf16[1,128,4096]{2,1,0:T(8,128)(2,1)S(1)}, bf16[1,128,4096]{2,1,0:T(8,128)(2,1)}, u32[]{:S(2)}) copy-start(bf16[1,128,4096]{2,1,0:T(8,128)(2,1)} %param.11) | copy-start | bytes 3145732

commit v3 on v2

--- a/solution.py
+++ b/solution.py
@@ -21,9 +21,15 @@
 SMALL_LIMIT = 12 * 1024 * 1024
 
 
-def member_order(count):
-    order = list(range(count))
-    random.Random(58).shuffle(order)
+def member_order(y_count, ctx_count, together):
+    draw = random.Random(31)
+    runs = list(range(ctx_count // together))
+    draw.shuffle(runs)
+    order = []
+    for run in runs:
+        members = [y * ctx_count + run * together + c for y in range(y_count) for c in range(together)]
+        draw.shuffle(members)
+        order += members
     return order
 
 
@@ -59,7 +65,8 @@
     q_hbm, k_hbm, v_hbm, u_hbm, out_hbm,
     q_ref, k_ref, v_ref, u_ref, out_ref, in_sem, out_sem, *, slots
 ):
-    half_rows = out_ref.shape[3]
+    half_rows = out_ref.shape[2]
+    together = BLOCK // (2 * half_rows)
     width = q_ref.shape[1] // CHUNKS
     count = width // BLOCK
     sources = ((q_hbm, q_ref), (k_hbm, k_ref), (v_hbm, v_ref), (u_hbm, u_ref))
@@ -78,17 +85,22 @@
                 kv = k_ref[:, lanes].astype(F32) * v_ref[:, lanes].astype(F32)
                 gg = u_ref[:, lanes].astype(F32) * q_ref[:, lanes].astype(F32)
                 for signal, value in enumerate((kv, gg)):
+                    value = value.astype(BF16)
                     parts = swap_halves(value[:half_rows], value[half_rows:])
                     for odd in range(2):
-                        out_ref[2 * pair + odd, block, signal] = parts[odd].astype(BF16)
-            for y, row in enumerate(slots):
-                copy = pltpu.make_async_copy(
-                    out_ref.at[y, block], out_hbm.at[row[block]], out_sem.at[row[block]]
-                )
-                copy.start()
-                stores.append(copy)
+                        out_ref[slots[2 * pair + odd][block], signal] = parts[odd]
+            if block % together == together - 1:
+                stores.append(send_run(out_ref, out_hbm, out_sem, slots, block // together, together))
     for copy in stores:
         copy.wait()
+
+
+def send_run(source, target, sem, slots, run, together):
+    places = [row[run * together + c] for row in slots for c in range(together)]
+    part = pl.ds(min(places), len(places))
+    copy = pltpu.make_async_copy(source.at[part], target.at[part], sem.at[run])
+    copy.start()
+    return copy
 
 
 def load_chunk(pairs, sem, chunk, width):
@@ -132,13 +144,13 @@
                 lanes = pl.ds(pair * LANES, LANES)
                 first, second = swap_halves(
                     *(
-                        arrived_ref[slots[2 * pair + odd][block * per_block + part], signal].astype(F32)
+                        arrived_ref[slots[2 * pair + odd][block * per_block + part], signal]
                         for odd in range(2)
                     )
                 )
                 at = part * 2 * half_rows
-                sig_ref[block, pl.ds(at, half_rows), lanes] = first.astype(BF16)
-                sig_ref[block, pl.ds(at + half_rows, half_rows), lanes] = second.astype(BF16)
+                sig_ref[block, pl.ds(at, half_rows), lanes] = first
+                sig_ref[block, pl.ds(at + half_rows, half_rows), lanes] = second
         spec_ref[block] = jnp.dot(forward_ref[...], sig_ref[block], preferred_element_type=F32)
 
 
@@ -190,10 +202,10 @@
     loads = filter_loads(filt_hbm, filt_ref, filt_sem)
     spectrum(arrived_ref, forward_ref, sig_ref, value_ref, slots, 0)
     spectrum(arrived_ref, forward_ref, sig_ref, grad_ref, slots, 1)
+    half = blocks // 2
     signs = row_signs((TILE, LANES))
 
-    def tile(step, carry):
-        where = tile_slices(step)
+    def cross_terms(where):
         value, grad = read_tiles(value_ref, where), read_tiles(grad_ref, where)
         window = [
             (grad[b][0] + signs * grad[b + 1][1], grad[b][1] - signs * grad[b + 1][0])
@@ -201,25 +213,28 @@
         ] + [grad[-1]]
         left = [(real - imag, real, imag) for real, imag in value]
         right = [side(*x) for x in window]
+        return [
+            multiply_conj([(left[j], right[b + j]) for j in range(blocks - b)]) for b in range(blocks)
+        ]
+
+    def tile(step, carry):
+        first, second = (cross_terms(tile_slices(2 * step + pair)) for pair in range(2))
+        real_rows, imag_rows, _ = tile_slices(2 * step)
         for b in range(blocks):
-            write_tile(
-                prod_ref, where, b, multiply_conj([(left[j], right[b + j]) for j in range(blocks - b)])
-            )
+            lanes = pl.ds(b // half * LANES, LANES)
+            real, imag = (first[b][i] + second[b][i] for i in range(2))
+            write_tile(prod_ref, (real_rows, imag_rows, lanes), b % half, (real, imag))
         return carry
 
-    lax.fori_loop(0, BLOCK // TILE * 2, tile, 0)
+    lax.fori_loop(0, BLOCK // TILE, tile, 0)
 
     mask = low_lanes((BLOCK, LANES))
-    folded = []
-    for block in range(blocks):
+    for block in range(half):
         cross = jnp.dot(inverse_ref[...], prod_ref[block], preferred_element_type=F32)
-        cross = cross[:, :LANES] + cross[:, LANES:]
-        folded.append(cross + pltpu.roll(cross, HALF, 1))
-        if block >= blocks // 2:
-            at = block - blocks // 2
-            terms_ref[pl.ds(at * BLOCK, BLOCK), :] = jnp.where(
-                mask, folded[at], folded[block]
-            ).astype(BF16)
+        early, late = (
+            part + pltpu.roll(part, HALF, 1) for part in (cross[:, :LANES], cross[:, LANES:])
+        )
+        terms_ref[pl.ds(block * BLOCK, BLOCK), :] = jnp.where(mask, early, late).astype(BF16)
     for copy in loads:
         copy.wait()
 
@@ -238,8 +253,7 @@
 def invert_block(inverse_ref, prod_ref, out_ref, block, slots, signal):
     half_rows = out_ref.shape[2]
     per_block = BLOCK // (2 * half_rows)
-    result = jnp.dot(inverse_ref[...], prod_ref[block], preferred_element_type=F32)
-    places = []
+    result = jnp.dot(inverse_ref[...], prod_ref[block], preferred_element_type=F32).astype(BF16)
     for part in range(per_block):
         at = part * 2 * half_rows
         for pair in range(2):
@@ -249,15 +263,14 @@
             )
             for odd in range(2):
                 place = slots[2 * pair + odd][block * per_block + part]
-                out_ref[place, signal] = parts[odd].astype(BF16)
-                places.append(place)
-    return places
+                out_ref[place, signal] = parts[odd]
 
 
 def conv_kernel(
     value_ref, grad_ref, filt_ref, inverse_ref, out_hbm, conv_ref, back_ref, out_ref, out_sem, *, slots
 ):
     blocks = value_ref.shape[0]
+    together = BLOCK // (2 * out_ref.shape[2])
 
     def tile(step, carry):
         where = tile_slices(step)
@@ -279,11 +292,8 @@
     stores = []
     for block in range(blocks):
         for signal, prod_ref in enumerate((conv_ref, back_ref)):
-            places = invert_block(inverse_ref, prod_ref, out_ref, block, slots, signal)
-        for place in places:
-            copy = pltpu.make_async_copy(out_ref.at[place], out_hbm.at[place], out_sem.at[place])
-            copy.start()
-            stores.append(copy)
+            invert_block(inverse_ref, prod_ref, out_ref, block, slots, signal)
+        stores.append(send_run(out_ref, out_hbm, out_sem, slots, block, together))
     for copy in stores:
         copy.wait()
 
@@ -302,15 +312,15 @@
                 lanes = pl.ds((block * 2 + pair) * LANES, LANES)
                 conv, back = (
                     swap_halves(
-                        *(ret_ref[slots[2 * pair + odd][block], signal].astype(F32) for odd in range(2))
+                        *(ret_ref[slots[2 * pair + odd][block], signal] for odd in range(2))
                     )
                     for signal in range(2)
                 )
                 for part in range(2):
                     rows = pl.ds(part * half_rows, half_rows)
-                    dq_ref[rows, lanes] = (u_ref[rows, lanes].astype(F32) * conv[part]).astype(BF16)
-                    dk_ref[rows, lanes] = (back[part] * v_ref[rows, lanes].astype(F32)).astype(BF16)
-                    dv_ref[rows, lanes] = (back[part] * k_ref[rows, lanes].astype(F32)).astype(BF16)
+                    dq_ref[rows, lanes] = (u_ref[rows, lanes].astype(F32) * conv[part].astype(F32)).astype(BF16)
+                    dk_ref[rows, lanes] = (back[part].astype(F32) * v_ref[rows, lanes].astype(F32)).astype(BF16)
+                    dv_ref[rows, lanes] = (back[part].astype(F32) * k_ref[rows, lanes].astype(F32)).astype(BF16)
         for copy in stores[chunk]:
             copy.start()
     for row in stores:
@@ -333,12 +343,9 @@
         part = pl.ds(chunk * step, step)
         for pair in range(2):
             lanes = pl.ds(pair * LANES, LANES)
-            values = swap_halves(
-                held_ref[2 * pair, part].astype(F32) * scale,
-                held_ref[2 * pair + 1, part].astype(F32) * scale,
-            )
+            values = swap_halves(held_ref[2 * pair, part], held_ref[2 * pair + 1, part])
             for half in range(2):
-                out_ref[pl.ds(half * rows + chunk * step, step), lanes] = values[half]
+                out_ref[pl.ds(half * rows + chunk * step, step), lanes] = values[half].astype(F32) * scale
         for half in range(2):
             part = pl.ds(half * rows + chunk * step, step)
             copy = pltpu.make_async_copy(out_ref.at[part], out_hbm.at[part], out_sem.at[half, chunk])
@@ -359,7 +366,7 @@
     params = pltpu.CompilerParams(vmem_limit_bytes=VMEM_LIMIT)
     upper, lower, inverse = (jnp.asarray(t) for t in dft_tables())
     members = y_count * ctx_count
-    order = member_order(members)
+    order = member_order(y_count, ctx_count, BLOCK // tokens)
     groups = [[z * members + m for m in order] for z in range(z_count)]
     place_of = [[order.index(y * ctx_count + c) for c in range(ctx_count)] for y in range(y_count)]
     hbm = pl.BlockSpec(memory_space=pltpu.HBM)
@@ -375,9 +382,9 @@
         out_shape=pltpu.HBM(packed_shape, BF16),
         scratch_shapes=[token_tile] * 4
         + [
-            pltpu.VMEM((y_count, ctx_count) + packed_shape[1:], BF16),
+            pltpu.VMEM(packed_shape, BF16),
             pltpu.SemaphoreType.DMA((4, CHUNKS)),
-            pltpu.SemaphoreType.DMA((members,)),
+            pltpu.SemaphoreType.DMA((blocks,)),
         ],
         compiler_params=params,
         name="gate",
@@ -420,7 +427,11 @@
             spectrum_shape,
             jax.ShapeDtypeStruct(filt.shape, F32),
         ],
-        scratch_shapes=[signal_tile, product_tile, pltpu.SemaphoreType.DMA((2, blocks))],
+        scratch_shapes=[
+            signal_tile,
+            pltpu.VMEM((blocks // 2, 2 * BLOCK, 2 * LANES), BF16),
+            pltpu.SemaphoreType.DMA((2, blocks)),
+        ],
         compiler_params=params,
         name="filter_terms",
     )(arrived, upper, inverse, filt)
@@ -433,7 +444,7 @@
             product_tile,
             product_tile,
             pltpu.VMEM(packed_shape, BF16),
-            pltpu.SemaphoreType.DMA((members,)),
+            pltpu.SemaphoreType.DMA((blocks,)),
         ],
         compiler_params=params,
         name="convolve",

time: 106 us -> 105 us (level)
  waiting for transfers between devices: 49.1 us -> 51.4 us
  starting transfers between devices: 25.4 us -> 23.4 us
  Pallas kernels: 25.9 us -> 24.4 us
    all_to_all x2, starting transfers between devices: 19.9 us -> 16.6 us  [exchange(): lax.all_to_all(array, ('seq', 'ctx'), 0, 0, tiled=True, axis_index_groups...]
    all_to_all x2, waiting for transfers between devices: 44.7 us -> 47.7 us  [exchange(): lax.all_to_all(array, ('seq', 'ctx'), 0, 0, tiled=True, axis_index_groups...]
    ppermute x3, starting transfers between devices: 2.15 us -> 3.33 us  [local(): lax.ppermute(summed, 'seq', [(s, s // y_count * y_count + (s + shift) % y...]
  transfers between devices with their start and end apart: 6 -> 6, of which waited for: 4 -> 5; matrix products, arithmetic and copies ran while one was open for 0% -> 0% of each run, Pallas kernels for 13% -> 12%
where the time goes in v3:
time: 105 us; the launch traced here: 104 us
  waiting for transfers between devices  51.4 us (49%)
  Pallas kernels  24.4 us (23%)
  starting transfers between devices  23.4 us (22%)
  local copies, waits for them, and re-layouts  4.06 us (4%)
    all_to_all x2, waiting for transfers between devices, exchange(): lax.all_to_all(array, ('seq', 'ctx'), 0, 0, tiled=True, axis_index_groups...  47.7 us
    all_to_all x2, starting transfers between devices, exchange(): lax.all_to_all(array, ('seq', 'ctx'), 0, 0, tiled=True, axis_index_groups...  16.6 us
    pallas_call x1, Pallas kernels, local(): pl.pallas_call(functools.partial(conv_kernel, slots=place_of), in_specs=[...  7.47 us
    pallas_call x1, Pallas kernels, local(): pl.pallas_call(functools.partial(cross_kernel, slots=place_of), in_specs=...  5.37 us
    unnamed x14, local copies, waits for them, and re-layouts  4.06 us
    ppermute x3, waiting for transfers between devices, local(): lax.ppermute(summed, 'seq', [(s, s // y_count * y_count + (s + shift) % y...  3.76 us
    pallas_call x1, Pallas kernels, local(): pl.pallas_call(functools.partial(gate_kernel, slots=place_of), in_specs=[...  3.42 us
    ppermute x1, starting transfers between devices, local(): lax.ppermute(part_grad, 'seq', [(s, (s + y_count) % seq_count) for s in r...  3.38 us
  transfers between devices with their start and end apart: 6, of which 5 were waited for; matrix products, arithmetic and copies ran while one was open for 0% of the time, Pallas kernels for 12%

profile of v3, /device:TPU:1, one launch (start us, length us, event | category | flops | bytes accessed | tf_op | source)
XLA Modules:
  0.0 104.0 jit_solution(147186708878749543)
XLA Ops:
  0.6 3.4 %gate.1 = bf16[64,2,64,128]{3,2,1,0:T(8,128)(2,1)} custom-call(bf16[128,4096]{1,0:T(8,128)(2,1)} %bitcast.15, bf16[128,4096]{1,0:T(8,128)(2,1)} %bitcast.8, bf16[128,4096]{1,0:T(8,128)(2,1)} %bitcast.10, bf16[128,4096]{1,0:T(8,128)(2,1)} %bitcast.12), custom_call_target="tpu_custom_call" | custom-call | tf_op jit(solution)/shard_map/gate/pallas_call | solution.py:378
  4.1 0.0 copy-start.5
  4.1 0.0 copy-start.6
  4.1 10.8 %all-to-all-start = ((bf16[64,2,64,128]{3,2,1,0:T(8,128)(2,1)}), bf16[64,2,64,128]{3,2,1,0:T(8,128)(2,1)S(1)}, u32[]{:S(2)}, u32[]{:S(2)}) async-start(bf16[64,2,64,128]{3,2,1,0:T(8,128)(2,1)} %gate.1), calls=%async_computation | async-start | bytes 4194304 | tf_op jit(solution)/shard_map/all_to_all | solution.py:394
  14.9 0.0 copy-done.5
  14.9 0.0 copy-done.6
  14.9 0.0 copy-start.3
  14.9 1.6 %copy-done.3 = f32[2048,256]{1,0:T(8,128)S(1)} copy-done((f32[2048,256]{1,0:T(8,128)S(1)}, f32[2048,256]{1,0:T(8,128)}, u32[]{:S(2)}) %copy-start.3) | copy-done | bytes 2097176
  16.5 0.0 copy-start.4
  16.5 3.2 %filter_spectra.1.filt_hbm = f32[2,8,256,128]{3,2,1,0:T(8,128)} custom-call(s32[1]{0:T(128)} %bitcast.4.place_ref, f32[2048,256]{1,0:T(8,128)S(1)} %copy-done.3, bf16[512,256]{1,0:T(8,128)(2,1)S(1)} %copy-done.5, bf16[512,256]{1,0:T(8,128)(2,1)S(1)} %copy-done.6), custom_call_target="tpu_custom_call" | custom-call | tf_op jit(solution)/shard_map/filter_spectra/pallas_call | solution.py:399
  19.8 22.8 %all-to-all-done.arrived_ref = bf16[64,2,64,128]{3,2,1,0:T(8,128)(2,1)S(1)} async-done(((bf16[64,2,64,128]{3,2,1,0:T(8,128)(2,1)}), bf16[64,2,64,128]{3,2,1,0:T(8,128)(2,1)S(1)}, u32[]{:S(2)}, u32[]{:S(2)}) %all-to-all-start) | async-done | bytes 2097184 | tf_op jit(solution)/shard_map/all_to_all | solution.py:394
  42.6 0.0 copy-done.4
  42.6 5.4 %filter_terms.1 = (bf16[1024,128]{1,0:T(8,128)(2,1)S(1)}, f32[8,512,256]{2,1,0:T(8,128)S(1)}, f32[8,512,256]{2,1,0:T(8,128)S(1)}, f32[2,8,256,128]{3,2,1,0:T(8,128)S(1)}) custom-call(bf16[64,2,64,128]{3,2,1,0:T(8,128)(2,1)S(1)} %all-to-all-done.arrived_ref, bf16[512,256]{1,0:T(8,128)(2,1)S(1)} %copy-done.5, bf16[256,512]{1,0:T(8,128)(2,1)S(1)} %copy-done.4, ...), custom_call_target="tpu_custom_call" | custom-call | tf_op jit(solution)/shard_map/filter_terms/pallas_call | solution.py:420
  48.0 3.4 %collective-permute-start = (bf16[1024,128]{1,0:T(8,128)(2,1)S(1)}, bf16[1024,128]{1,0:T(8,128)(2,1)S(1)}, u32[]{:S(2)}, u32[]{:S(2)}) collective-permute-start(bf16[1024,128]{1,0:T(8,128)(2,1)S(1)} %get-tuple-element.16), channel_id=1, source_target_pairs={{0,64},{16,80},{32,96},{48,112},{64,0},{80,16},{96,32},{112,48},{1... | collective-permute-start | bytes 786440 | tf_op jit(solution)/shard_map/ppermute | solution.py:452
  51.4 7.5 %convolve.1 = bf16[64,2,64,128]{3,2,1,0:T(8,128)(2,1)} custom-call(f32[8,512,256]{2,1,0:T(8,128)S(1)} %get-tuple-element.13.value_ref, f32[8,512,256]{2,1,0:T(8,128)S(1)} %get-tuple-element.14.grad_ref, f32[2,8,256,128]{3,2,1,0:T(8,128)S(1)} %get-tuple-element.15.filt_ref, bf16[256,512]{1,0:T(8,128)(2,1)S(1)} %copy-done.4), custom_call_target="tpu_custom_call" | custom-call | tf_op jit(solution)/shard_map/convolve/pallas_call | solution.py:438
  58.8 0.0 collective-permute-done
  58.8 0.1 add_convert_fusion.own_ref
  58.9 0.0 copy-start
  58.9 5.8 %all-to-all-start.1 = ((bf16[64,2,64,128]{3,2,1,0:T(8,128)(2,1)}), bf16[64,2,64,128]{3,2,1,0:T(8,128)(2,1)S(1)}, u32[]{:S(2)}, u32[]{:S(2)}) async-start(bf16[64,2,64,128]{3,2,1,0:T(8,128)(2,1)} %convolve.1), calls=%async_computation.1 | async-start | bytes 4194304 | tf_op jit(solution)/shard_map/all_to_all | solution.py:394
  64.8 1.9 %collective-permute-start.3 = (bf16[1024,128]{1,0:T(8,128)(2,1)S(1)}, bf16[1024,128]{1,0:T(8,128)(2,1)}, u32[]{:S(2)}, u32[]{:S(2)}) collective-permute-start(bf16[1024,128]{1,0:T(8,128)(2,1)S(1)} %add_convert_fusion.own_ref), channel_id=1, source_target_pairs={{0,32},{16,48},{32,0},{48,16},{64,96},{80,112},{96,64},{112,80},{1... | collective-permute-start | bytes 786440 | tf_op jit(solution)/shard_map/ppermute | solution.py:458
  66.6 0.9 collective-permute-start.2
  67.6 0.6 collective-permute-start.1
  68.1 24.8 %all-to-all-done.1.ret_ref = bf16[64,2,64,128]{3,2,1,0:T(8,128)(2,1)S(1)} async-done(((bf16[64,2,64,128]{3,2,1,0:T(8,128)(2,1)}), bf16[64,2,64,128]{3,2,1,0:T(8,128)(2,1)S(1)}, u32[]{:S(2)}, u32[]{:S(2)}) %all-to-all-start.1) | async-done | bytes 2097184 | tf_op jit(solution)/shard_map/all_to_all | solution.py:394
  92.9 0.0 copy-done
  92.9 0.0 copy-start.1
  92.9 1.2 %copy-done.1 = bf16[1,128,4096]{2,1,0:T(8,128)(2,1)S(1)} copy-done((bf16[1,128,4096]{2,1,0:T(8,128)(2,1)S(1)}, bf16[1,128,4096]{2,1,0:T(8,128)(2,1)}, u32[]{:S(2)}) %copy-start.1) | copy-done | bytes 1048600
  94.2 0.0 copy-start.2
  94.2 1.2 %copy-done.2 = bf16[1,128,4096]{2,1,0:T(8,128)(2,1)S(1)} copy-done((bf16[1,128,4096]{2,1,0:T(8,128)(2,1)S(1)}, bf16[1,128,4096]{2,1,0:T(8,128)(2,1)}, u32[]{:S(2)}) %copy-start.2) | copy-done | bytes 1048600
  95.4 2.1 %products.1 = (bf16[128,4096]{1,0:T(8,128)(2,1)}, bf16[128,4096]{1,0:T(8,128)(2,1)}, bf16[128,4096]{1,0:T(8,128)(2,1)}) custom-call(bf16[64,2,64,128]{3,2,1,0:T(8,128)(2,1)S(1)} %all-to-all-done.1.ret_ref, bf16[128,4096]{1,0:T(8,128)(2,1)S(1)} %bitcast.9, bf16[128,4096]{1,0:T(8,128)(2,1)S(1)} %bitcast.11, bf16[128,4096]{1,0:T(8,128)(2,1)S(1)} %bitcast.13), custom_call_target="tpu_custom_call" | custom-call | tf_op jit(solution)/shard_map/products/pallas_call | solution.py:466
  97.5 0.6 collective-permute-done.3.far_ref
  98.1 2.0 %collective-permute-done.2.down_ref = bf16[1024,128]{1,0:T(8,128)(2,1)} collective-permute-done((bf16[1024,128]{1,0:T(8,128)(2,1)S(1)}, bf16[1024,128]{1,0:T(8,128)(2,1)}, u32[]{:S(2)}, u32[]{:S(2)}) %collective-permute-start.2) | collective-permute-done | bytes 262176 | tf_op jit(solution)/shard_map/ppermute | solution.py:458
  100.1 1.2 %collective-permute-done.1.up_ref = bf16[1024,128]{1,0:T(8,128)(2,1)} collective-permute-done((bf16[1024,128]{1,0:T(8,128)(2,1)S(1)}, bf16[1024,128]{1,0:T(8,128)(2,1)}, u32[]{:S(2)}, u32[]{:S(2)}) %collective-permute-start.1) | collective-permute-done | bytes 262176 | tf_op jit(solution)/shard_map/ppermute | solution.py:458
  101.3 2.7 %spread.1 = f32[2048,256]{1,0:T(8,128)} custom-call(s32[1]{0:T(128)} %bitcast.4.place_ref, bf16[1024,128]{1,0:T(8,128)(2,1)S(1)} %add_convert_fusion.own_ref, bf16[1024,128]{1,0:T(8,128)(2,1)} %collective-permute-done.1.up_ref, bf16[1024,128]{1,0:T(8,128)(2,1)} %collective-permute-done.2.down_ref, bf16[1024,128]{1,0:T(8,128)(2,1)} %collective-permute-done.3.far_ref, ...), custom_call_target="tpu_custom_call" | custom-call | tf_op jit(solution)/shard_map/spread/pallas_call | solution.py:475
Async XLA Ops:
  4.1 10.8 %copy-start.5 = (bf16[512,256]{1,0:T(8,128)(2,1)S(1)}, bf16[512,256]{1,0:T(8,128)(2,1)}, u32[]{:S(2)}) copy-start(bf16[512,256]{1,0:T(8,128)(2,1)} %constant.17.clone.upper_ref.forward_ref) | copy-start | bytes 786436
  4.1 10.8 %copy-start.6 = (bf16[512,256]{1,0:T(8,128)(2,1)S(1)}, bf16[512,256]{1,0:T(8,128)(2,1)}, u32[]{:S(2)}) copy-start(bf16[512,256]{1,0:T(8,128)(2,1)} %constant.18.clone.lower_ref) | copy-start | bytes 786436
  4.1 38.5 %all-to-all-start = ((bf16[64,2,64,128]{3,2,1,0:T(8,128)(2,1)}), bf16[64,2,64,128]{3,2,1,0:T(8,128)(2,1)S(1)}, u32[]{:S(2)}, u32[]{:S(2)}) async-start(bf16[64,2,64,128]{3,2,1,0:T(8,128)(2,1)} %gate.1), calls=%async_computation | async-start | bytes 4194304 | tf_op jit(solution)/shard_map/all_to_all | solution.py:394
  14.9 1.6 %copy-start.3 = (f32[2048,256]{1,0:T(8,128)S(1)}, f32[2048,256]{1,0:T(8,128)}, u32[]{:S(2)}) copy-start(f32[2048,256]{1,0:T(8,128)} %taps_ref.1) | copy-start | bytes 6291460
  16.5 26.1 %copy-start.4 = (bf16[256,512]{1,0:T(8,128)(2,1)S(1)}, bf16[256,512]{1,0:T(8,128)(2,1)}, u32[]{:S(2)}) copy-start(bf16[256,512]{1,0:T(8,128)(2,1)} %constant.19.clone.inverse_ref) | copy-start | bytes 786436
  48.0 10.9 %collective-permute-start = (bf16[1024,128]{1,0:T(8,128)(2,1)S(1)}, bf16[1024,128]{1,0:T(8,128)(2,1)S(1)}, u32[]{:S(2)}, u32[]{:S(2)}) collective-permute-start(bf16[1024,128]{1,0:T(8,128)(2,1)S(1)} %get-tuple-element.16), channel_id=1, source_target_pairs={{0,64},{16,80},{32,96},{48,112},{64,0},{80,16},{96,32},{112,48},{1... | collective-permute-start | bytes 786440 | tf_op jit(solution)/shard_map/ppermute | solution.py:452
  58.9 34.0 %copy-start = (bf16[1,128,4096]{2,1,0:T(8,128)(2,1)S(1)}, bf16[1,128,4096]{2,1,0:T(8,128)(2,1)}, u32[]{:S(2)}) copy-start(bf16[1,128,4096]{2,1,0:T(8,128)(2,1)} %param.9) | copy-start | bytes 3145732
  58.9 34.0 %all-to-all-start.1 = ((bf16[64,2,64,128]{3,2,1,0:T(8,128)(2,1)}), bf16[64,2,64,128]{3,2,1,0:T(8,128)(2,1)S(1)}, u32[]{:S(2)}, u32[]{:S(2)}) async-start(bf16[64,2,64,128]{3,2,1,0:T(8,128)(2,1)} %convolve.1), calls=%async_computation.1 | async-start | bytes 4194304 | tf_op jit(solution)/shard_map/all_to_all | solution.py:394
  64.8 33.3 %collective-permute-start.3 = (bf16[1024,128]{1,0:T(8,128)(2,1)S(1)}, bf16[1024,128]{1,0:T(8,128)(2,1)}, u32[]{:S(2)}, u32[]{:S(2)}) collective-permute-start(bf16[1024,128]{1,0:T(8,128)(2,1)S(1)} %add_convert_fusion.own_ref), channel_id=1, source_target_pairs={{0,32},{16,48},{32,0},{48,16},{64,96},{80,112},{96,64},{112,80},{1... | collective-permute-start | bytes 786440 | tf_op jit(solution)/shard_map/ppermute | solution.py:458
  66.6 33.5 %collective-permute-start.2 = (bf16[1024,128]{1,0:T(8,128)(2,1)S(1)}, bf16[1024,128]{1,0:T(8,128)(2,1)}, u32[]{:S(2)}, u32[]{:S(2)}) collective-permute-start(bf16[1024,128]{1,0:T(8,128)(2,1)S(1)} %add_convert_fusion.own_ref), channel_id=1, source_target_pairs={{0,48},{16,0},{32,16},{48,32},{64,112},{80,64},{96,80},{112,96},{1... | collective-permute-start | bytes 786440 | tf_op jit(solution)/shard_map/ppermute | solution.py:458
  67.6 33.7 %collective-permute-start.1 = (bf16[1024,128]{1,0:T(8,128)(2,1)S(1)}, bf16[1024,128]{1,0:T(8,128)(2,1)}, u32[]{:S(2)}, u32[]{:S(2)}) collective-permute-start(bf16[1024,128]{1,0:T(8,128)(2,1)S(1)} %add_convert_fusion.own_ref), channel_id=1, source_target_pairs={{0,16},{16,32},{32,48},{48,0},{64,80},{80,96},{96,112},{112,64},{1... | collective-permute-start | bytes 786440 | tf_op jit(solution)/shard_map/ppermute | solution.py:458
  92.9 1.2 %copy-start.1 = (bf16[1,128,4096]{2,1,0:T(8,128)(2,1)S(1)}, bf16[1,128,4096]{2,1,0:T(8,128)(2,1)}, u32[]{:S(2)}) copy-start(bf16[1,128,4096]{2,1,0:T(8,128)(2,1)} %param.10) | copy-start | bytes 3145732
  94.2 1.2 %copy-start.2 = (bf16[1,128,4096]{2,1,0:T(8,128)(2,1)S(1)}, bf16[1,128,4096]{2,1,0:T(8,128)(2,1)}, u32[]{:S(2)}) copy-start(bf16[1,128,4096]{2,1,0:T(8,128)(2,1)} %param.11) | copy-start | bytes 3145732

commit v4 on v3

--- a/solution.py
+++ b/solution.py
@@ -22,7 +22,7 @@
 
 
 def member_order(y_count, ctx_count, together):
-    draw = random.Random(31)
+    draw = random.Random(44)
     runs = list(range(ctx_count // together))
     draw.shuffle(runs)
     order = []

time: 105 us -> 104 us (level)
  waiting for transfers between devices: 51.4 us -> 47.6 us
  starting transfers between devices: 23.4 us -> 26.3 us
    all_to_all x2, waiting for transfers between devices: 47.7 us -> 42.3 us  [exchange(): lax.all_to_all(array, ('seq', 'ctx'), 0, 0, tiled=True, axis_index_groups...]
    all_to_all x2, starting transfers between devices: 16.6 us -> 20.8 us  [exchange(): lax.all_to_all(array, ('seq', 'ctx'), 0, 0, tiled=True, axis_index_groups...]
    ppermute x3, waiting for transfers between devices: 3.76 us -> 5.31 us  [local(): lax.ppermute(summed, 'seq', [(s, s // y_count * y_count + (s + shift) % y...]
    ppermute x3, starting transfers between devices: 3.33 us -> 2.18 us  [local(): lax.ppermute(summed, 'seq', [(s, s // y_count * y_count + (s + shift) % y...]
where the time goes in v4:
time: 104 us; the launch traced here: 103 us
  waiting for transfers between devices  47.6 us (46%)
  starting transfers between devices  26.3 us (25%)
  Pallas kernels  24.3 us (23%)
  local copies, waits for them, and re-layouts  4.06 us (4%)
    all_to_all x2, waiting for transfers between devices, exchange(): lax.all_to_all(array, ('seq', 'ctx'), 0, 0, tiled=True, axis_index_groups...  42.3 us
    all_to_all x2, starting transfers between devices, exchange(): lax.all_to_all(array, ('seq', 'ctx'), 0, 0, tiled=True, axis_index_groups...  20.8 us
    pallas_call x1, Pallas kernels, local(): pl.pallas_call(functools.partial(conv_kernel, slots=place_of), in_specs=[...  7.46 us
    pallas_call x1, Pallas kernels, local(): pl.pallas_call(functools.partial(cross_kernel, slots=place_of), in_specs=...  5.37 us
    ppermute x3, waiting for transfers between devices, local(): lax.ppermute(summed, 'seq', [(s, s // y_count * y_count + (s + shift) % y...  5.31 us
    unnamed x14, local copies, waits for them, and re-layouts  4.06 us
    pallas_call x1, Pallas kernels, local(): pl.pallas_call(functools.partial(gate_kernel, slots=place_of), in_specs=[...  3.42 us
    ppermute x1, starting transfers between devices, local(): lax.ppermute(part_grad, 'seq', [(s, (s + y_count) % seq_count) for s in r...  3.38 us
  transfers between devices with their start and end apart: 6, of which 5 were waited for; matrix products, arithmetic and copies ran while one was open for 0% of the time, Pallas kernels for 12%

profile of v4, /device:TPU:1, one launch (start us, length us, event | category | flops | bytes accessed | tf_op | source)
XLA Modules:
  0.0 103.2 jit_solution(334381795042148559)
XLA Ops:
  0.6 3.4 %gate.1 = bf16[64,2,64,128]{3,2,1,0:T(8,128)(2,1)} custom-call(bf16[128,4096]{1,0:T(8,128)(2,1)} %bitcast.15, bf16[128,4096]{1,0:T(8,128)(2,1)} %bitcast.8, bf16[128,4096]{1,0:T(8,128)(2,1)} %bitcast.10, bf16[128,4096]{1,0:T(8,128)(2,1)} %bitcast.12), custom_call_target="tpu_custom_call" | custom-call | tf_op jit(solution)/shard_map/gate/pallas_call | solution.py:378
  4.1 0.0 copy-start.5
  4.1 0.0 copy-start.6
  4.1 11.8 %all-to-all-start = ((bf16[64,2,64,128]{3,2,1,0:T(8,128)(2,1)}), bf16[64,2,64,128]{3,2,1,0:T(8,128)(2,1)S(1)}, u32[]{:S(2)}, u32[]{:S(2)}) async-start(bf16[64,2,64,128]{3,2,1,0:T(8,128)(2,1)} %gate.1), calls=%async_computation | async-start | bytes 4194304 | tf_op jit(solution)/shard_map/all_to_all | solution.py:394
  15.9 0.0 copy-done.5
  16.0 0.0 copy-done.6
  16.0 0.0 copy-start.3
  16.0 1.6 %copy-done.3 = f32[2048,256]{1,0:T(8,128)S(1)} copy-done((f32[2048,256]{1,0:T(8,128)S(1)}, f32[2048,256]{1,0:T(8,128)}, u32[]{:S(2)}) %copy-start.3) | copy-done | bytes 2097176
  17.6 0.0 copy-start.4
  17.6 3.2 %filter_spectra.1.filt_hbm = f32[2,8,256,128]{3,2,1,0:T(8,128)} custom-call(s32[1]{0:T(128)} %bitcast.4.place_ref, f32[2048,256]{1,0:T(8,128)S(1)} %copy-done.3, bf16[512,256]{1,0:T(8,128)(2,1)S(1)} %copy-done.5, bf16[512,256]{1,0:T(8,128)(2,1)S(1)} %copy-done.6), custom_call_target="tpu_custom_call" | custom-call | tf_op jit(solution)/shard_map/filter_spectra/pallas_call | solution.py:399
  20.8 19.8 %all-to-all-done.arrived_ref = bf16[64,2,64,128]{3,2,1,0:T(8,128)(2,1)S(1)} async-done(((bf16[64,2,64,128]{3,2,1,0:T(8,128)(2,1)}), bf16[64,2,64,128]{3,2,1,0:T(8,128)(2,1)S(1)}, u32[]{:S(2)}, u32[]{:S(2)}) %all-to-all-start) | async-done | bytes 2097184 | tf_op jit(solution)/shard_map/all_to_all | solution.py:394
  40.6 0.0 copy-done.4
  40.6 5.4 %filter_terms.1 = (bf16[1024,128]{1,0:T(8,128)(2,1)S(1)}, f32[8,512,256]{2,1,0:T(8,128)S(1)}, f32[8,512,256]{2,1,0:T(8,128)S(1)}, f32[2,8,256,128]{3,2,1,0:T(8,128)S(1)}) custom-call(bf16[64,2,64,128]{3,2,1,0:T(8,128)(2,1)S(1)} %all-to-all-done.arrived_ref, bf16[512,256]{1,0:T(8,128)(2,1)S(1)} %copy-done.5, bf16[256,512]{1,0:T(8,128)(2,1)S(1)} %copy-done.4, ...), custom_call_target="tpu_custom_call" | custom-call | tf_op jit(solution)/shard_map/filter_terms/pallas_call | solution.py:420
  46.0 3.4 %collective-permute-start = (bf16[1024,128]{1,0:T(8,128)(2,1)S(1)}, bf16[1024,128]{1,0:T(8,128)(2,1)S(1)}, u32[]{:S(2)}, u32[]{:S(2)}) collective-permute-start(bf16[1024,128]{1,0:T(8,128)(2,1)S(1)} %get-tuple-element.16), channel_id=1, source_target_pairs={{0,64},{16,80},{32,96},{48,112},{64,0},{80,16},{96,32},{112,48},{1... | collective-permute-start | bytes 786440 | tf_op jit(solution)/shard_map/ppermute | solution.py:452
  49.3 7.5 %convolve.1 = bf16[64,2,64,128]{3,2,1,0:T(8,128)(2,1)} custom-call(f32[8,512,256]{2,1,0:T(8,128)S(1)} %get-tuple-element.13.value_ref, f32[8,512,256]{2,1,0:T(8,128)S(1)} %get-tuple-element.14.grad_ref, f32[2,8,256,128]{3,2,1,0:T(8,128)S(1)} %get-tuple-element.15.filt_ref, bf16[256,512]{1,0:T(8,128)(2,1)S(1)} %copy-done.4), custom_call_target="tpu_custom_call" | custom-call | tf_op jit(solution)/shard_map/convolve/pallas_call | solution.py:438
  56.8 0.0 collective-permute-done
  56.8 0.1 add_convert_fusion.own_ref
  56.9 0.0 copy-start
  56.9 8.9 %all-to-all-start.1 = ((bf16[64,2,64,128]{3,2,1,0:T(8,128)(2,1)}), bf16[64,2,64,128]{3,2,1,0:T(8,128)(2,1)S(1)}, u32[]{:S(2)}, u32[]{:S(2)}) async-start(bf16[64,2,64,128]{3,2,1,0:T(8,128)(2,1)} %convolve.1), calls=%async_computation.1 | async-start | bytes 4194304 | tf_op jit(solution)/shard_map/all_to_all | solution.py:394
  65.8 0.4 collective-permute-start.3
  66.2 1.8 %collective-permute-start.2 = (bf16[1024,128]{1,0:T(8,128)(2,1)S(1)}, bf16[1024,128]{1,0:T(8,128)(2,1)}, u32[]{:S(2)}, u32[]{:S(2)}) collective-permute-start(bf16[1024,128]{1,0:T(8,128)(2,1)S(1)} %add_convert_fusion.own_ref), channel_id=1, source_target_pairs={{0,48},{16,0},{32,16},{48,32},{64,112},{80,64},{96,80},{112,96},{1... | collective-permute-start | bytes 786440 | tf_op jit(solution)/shard_map/ppermute | solution.py:458
  68.0 0.0 collective-permute-start.1
  68.0 22.6 %all-to-all-done.1.ret_ref = bf16[64,2,64,128]{3,2,1,0:T(8,128)(2,1)S(1)} async-done(((bf16[64,2,64,128]{3,2,1,0:T(8,128)(2,1)}), bf16[64,2,64,128]{3,2,1,0:T(8,128)(2,1)S(1)}, u32[]{:S(2)}, u32[]{:S(2)}) %all-to-all-start.1) | async-done | bytes 2097184 | tf_op jit(solution)/shard_map/all_to_all | solution.py:394
  90.6 0.0 copy-done
  90.6 0.0 copy-start.1
  90.6 1.2 %copy-done.1 = bf16[1,128,4096]{2,1,0:T(8,128)(2,1)S(1)} copy-done((bf16[1,128,4096]{2,1,0:T(8,128)(2,1)S(1)}, bf16[1,128,4096]{2,1,0:T(8,128)(2,1)}, u32[]{:S(2)}) %copy-start.1) | copy-done | bytes 1048600
  91.8 0.0 copy-start.2
  91.8 1.2 %copy-done.2 = bf16[1,128,4096]{2,1,0:T(8,128)(2,1)S(1)} copy-done((bf16[1,128,4096]{2,1,0:T(8,128)(2,1)S(1)}, bf16[1,128,4096]{2,1,0:T(8,128)(2,1)}, u32[]{:S(2)}) %copy-start.2) | copy-done | bytes 1048600
  93.0 2.1 %products.1 = (bf16[128,4096]{1,0:T(8,128)(2,1)}, bf16[128,4096]{1,0:T(8,128)(2,1)}, bf16[128,4096]{1,0:T(8,128)(2,1)}) custom-call(bf16[64,2,64,128]{3,2,1,0:T(8,128)(2,1)S(1)} %all-to-all-done.1.ret_ref, bf16[128,4096]{1,0:T(8,128)(2,1)S(1)} %bitcast.9, bf16[128,4096]{1,0:T(8,128)(2,1)S(1)} %bitcast.11, bf16[128,4096]{1,0:T(8,128)(2,1)S(1)} %bitcast.13), custom_call_target="tpu_custom_call" | custom-call | tf_op jit(solution)/shard_map/products/pallas_call | solution.py:466
  95.1 0.6 collective-permute-done.3.far_ref
  95.8 4.3 %collective-permute-done.2.down_ref = bf16[1024,128]{1,0:T(8,128)(2,1)} collective-permute-done((bf16[1024,128]{1,0:T(8,128)(2,1)S(1)}, bf16[1024,128]{1,0:T(8,128)(2,1)}, u32[]{:S(2)}, u32[]{:S(2)}) %collective-permute-start.2) | collective-permute-done | bytes 262176 | tf_op jit(solution)/shard_map/ppermute | solution.py:458
  100.1 0.4 collective-permute-done.1.up_ref
  100.5 2.7 %spread.1 = f32[2048,256]{1,0:T(8,128)} custom-call(s32[1]{0:T(128)} %bitcast.4.place_ref, bf16[1024,128]{1,0:T(8,128)(2,1)S(1)} %add_convert_fusion.own_ref, bf16[1024,128]{1,0:T(8,128)(2,1)} %collective-permute-done.1.up_ref, bf16[1024,128]{1,0:T(8,128)(2,1)} %collective-permute-done.2.down_ref, bf16[1024,128]{1,0:T(8,128)(2,1)} %collective-permute-done.3.far_ref, ...), custom_call_target="tpu_custom_call" | custom-call | tf_op jit(solution)/shard_map/spread/pallas_call | solution.py:475
Async XLA Ops:
  4.1 11.9 %copy-start.5 = (bf16[512,256]{1,0:T(8,128)(2,1)S(1)}, bf16[512,256]{1,0:T(8,128)(2,1)}, u32[]{:S(2)}) copy-start(bf16[512,256]{1,0:T(8,128)(2,1)} %constant.17.clone.upper_ref.forward_ref) | copy-start | bytes 786436
  4.1 11.9 %copy-start.6 = (bf16[512,256]{1,0:T(8,128)(2,1)S(1)}, bf16[512,256]{1,0:T(8,128)(2,1)}, u32[]{:S(2)}) copy-start(bf16[512,256]{1,0:T(8,128)(2,1)} %constant.18.clone.lower_ref) | copy-start | bytes 786436
  4.1 36.5 %all-to-all-start = ((bf16[64,2,64,128]{3,2,1,0:T(8,128)(2,1)}), bf16[64,2,64,128]{3,2,1,0:T(8,128)(2,1)S(1)}, u32[]{:S(2)}, u32[]{:S(2)}) async-start(bf16[64,2,64,128]{3,2,1,0:T(8,128)(2,1)} %gate.1), calls=%async_computation | async-start | bytes 4194304 | tf_op jit(solution)/shard_map/all_to_all | solution.py:394
  16.0 1.6 %copy-start.3 = (f32[2048,256]{1,0:T(8,128)S(1)}, f32[2048,256]{1,0:T(8,128)}, u32[]{:S(2)}) copy-start(f32[2048,256]{1,0:T(8,128)} %taps_ref.1) | copy-start | bytes 6291460
  17.6 23.0 %copy-start.4 = (bf16[256,512]{1,0:T(8,128)(2,1)S(1)}, bf16[256,512]{1,0:T(8,128)(2,1)}, u32[]{:S(2)}) copy-start(bf16[256,512]{1,0:T(8,128)(2,1)} %constant.19.clone.inverse_ref) | copy-start | bytes 786436
  46.0 10.9 %collective-permute-start = (bf16[1024,128]{1,0:T(8,128)(2,1)S(1)}, bf16[1024,128]{1,0:T(8,128)(2,1)S(1)}, u32[]{:S(2)}, u32[]{:S(2)}) collective-permute-start(bf16[1024,128]{1,0:T(8,128)(2,1)S(1)} %get-tuple-element.16), channel_id=1, source_target_pairs={{0,64},{16,80},{32,96},{48,112},{64,0},{80,16},{96,32},{112,48},{1... | collective-permute-start | bytes 786440 | tf_op jit(solution)/shard_map/ppermute | solution.py:452
  56.9 33.7 %copy-start = (bf16[1,128,4096]{2,1,0:T(8,128)(2,1)S(1)}, bf16[1,128,4096]{2,1,0:T(8,128)(2,1)}, u32[]{:S(2)}) copy-start(bf16[1,128,4096]{2,1,0:T(8,128)(2,1)} %param.9) | copy-start | bytes 3145732
  56.9 33.7 %all-to-all-start.1 = ((bf16[64,2,64,128]{3,2,1,0:T(8,128)(2,1)}), bf16[64,2,64,128]{3,2,1,0:T(8,128)(2,1)S(1)}, u32[]{:S(2)}, u32[]{:S(2)}) async-start(bf16[64,2,64,128]{3,2,1,0:T(8,128)(2,1)} %convolve.1), calls=%async_computation.1 | async-start | bytes 4194304 | tf_op jit(solution)/shard_map/all_to_all | solution.py:394
  65.8 29.9 %collective-permute-start.3 = (bf16[1024,128]{1,0:T(8,128)(2,1)S(1)}, bf16[1024,128]{1,0:T(8,128)(2,1)}, u32[]{:S(2)}, u32[]{:S(2)}) collective-permute-start(bf16[1024,128]{1,0:T(8,128)(2,1)S(1)} %add_convert_fusion.own_ref), channel_id=1, source_target_pairs={{0,32},{16,48},{32,0},{48,16},{64,96},{80,112},{96,64},{112,80},{1... | collective-permute-start | bytes 786440 | tf_op jit(solution)/shard_map/ppermute | solution.py:458
  66.2 33.9 %collective-permute-start.2 = (bf16[1024,128]{1,0:T(8,128)(2,1)S(1)}, bf16[1024,128]{1,0:T(8,128)(2,1)}, u32[]{:S(2)}, u32[]{:S(2)}) collective-permute-start(bf16[1024,128]{1,0:T(8,128)(2,1)S(1)} %add_convert_fusion.own_ref), channel_id=1, source_target_pairs={{0,48},{16,0},{32,16},{48,32},{64,112},{80,64},{96,80},{112,96},{1... | collective-permute-start | bytes 786440 | tf_op jit(solution)/shard_map/ppermute | solution.py:458
  68.0 32.5 %collective-permute-start.1 = (bf16[1024,128]{1,0:T(8,128)(2,1)S(1)}, bf16[1024,128]{1,0:T(8,128)(2,1)}, u32[]{:S(2)}, u32[]{:S(2)}) collective-permute-start(bf16[1024,128]{1,0:T(8,128)(2,1)S(1)} %add_convert_fusion.own_ref), channel_id=1, source_target_pairs={{0,16},{16,32},{32,48},{48,0},{64,80},{80,96},{96,112},{112,64},{1... | collective-permute-start | bytes 786440 | tf_op jit(solution)/shard_map/ppermute | solution.py:458
  90.6 1.2 %copy-start.1 = (bf16[1,128,4096]{2,1,0:T(8,128)(2,1)S(1)}, bf16[1,128,4096]{2,1,0:T(8,128)(2,1)}, u32[]{:S(2)}) copy-start(bf16[1,128,4096]{2,1,0:T(8,128)(2,1)} %param.10) | copy-start | bytes 3145732
  91.8 1.2 %copy-start.2 = (bf16[1,128,4096]{2,1,0:T(8,128)(2,1)S(1)}, bf16[1,128,4096]{2,1,0:T(8,128)(2,1)}, u32[]{:S(2)}) copy-start(bf16[1,128,4096]{2,1,0:T(8,128)(2,1)} %param.11) | copy-start | bytes 3145732

commit v5 on v4

--- a/solution.py
+++ b/solution.py
@@ -15,7 +15,7 @@
 LANES = 128
 F32 = jnp.float32
 BF16 = jnp.bfloat16
-TILE = 16
+TILE = 32
 CHUNKS = 4
 VMEM_LIMIT = 24 * 1024 * 1024
 SMALL_LIMIT = 12 * 1024 * 1024

time: 104 us -> 103 us (level)
  no operation moved by 1% of the time
where the time goes in v5:
time: 103 us; the launch traced here: 102 us
  waiting for transfers between devices  47.6 us (46%)
  starting transfers between devices  26.3 us (26%)
  Pallas kernels  23.4 us (23%)
  local copies, waits for them, and re-layouts  4.06 us (4%)
    all_to_all x2, waiting for transfers between devices, exchange(): lax.all_to_all(array, ('seq', 'ctx'), 0, 0, tiled=True, axis_index_groups...  42.3 us
    all_to_all x2, starting transfers between devices, exchange(): lax.all_to_all(array, ('seq', 'ctx'), 0, 0, tiled=True, axis_index_groups...  20.8 us
    pallas_call x1, Pallas kernels, local(): pl.pallas_call(functools.partial(conv_kernel, slots=place_of), in_specs=[...  6.99 us
    ppermute x3, waiting for transfers between devices, local(): lax.ppermute(summed, 'seq', [(s, s // y_count * y_count + (s + shift) % y...  5.31 us
    pallas_call x1, Pallas kernels, local(): pl.pallas_call(functools.partial(cross_kernel, slots=place_of), in_specs=...  4.93 us
    unnamed x14, local copies, waits for them, and re-layouts  4.06 us
    pallas_call x1, Pallas kernels, local(): pl.pallas_call(functools.partial(gate_kernel, slots=place_of), in_specs=[...  3.42 us
    ppermute x1, starting transfers between devices, local(): lax.ppermute(part_grad, 'seq', [(s, (s + y_count) % seq_count) for s in r...  3.38 us
  transfers between devices with their start and end apart: 6, of which 5 were waited for; matrix products, arithmetic and copies ran while one was open for 0% of the time, Pallas kernels for 12%

profile of v5, /device:TPU:1, one launch (start us, length us, event | category | flops | bytes accessed | tf_op | source)
XLA Modules:
  0.0 102.3 jit_solution(14395409366914206423)
XLA Ops:
  0.6 3.4 %gate.1 = bf16[64,2,64,128]{3,2,1,0:T(8,128)(2,1)} custom-call(bf16[128,4096]{1,0:T(8,128)(2,1)} %bitcast.15, bf16[128,4096]{1,0:T(8,128)(2,1)} %bitcast.8, bf16[128,4096]{1,0:T(8,128)(2,1)} %bitcast.10, bf16[128,4096]{1,0:T(8,128)(2,1)} %bitcast.12), custom_call_target="tpu_custom_call" | custom-call | tf_op jit(solution)/shard_map/gate/pallas_call | solution.py:378
  4.1 0.0 copy-start.5
  4.1 0.0 copy-start.6
  4.1 11.8 %all-to-all-start = ((bf16[64,2,64,128]{3,2,1,0:T(8,128)(2,1)}), bf16[64,2,64,128]{3,2,1,0:T(8,128)(2,1)S(1)}, u32[]{:S(2)}, u32[]{:S(2)}) async-start(bf16[64,2,64,128]{3,2,1,0:T(8,128)(2,1)} %gate.1), calls=%async_computation | async-start | bytes 4194304 | tf_op jit(solution)/shard_map/all_to_all | solution.py:394
  15.9 0.0 copy-done.5
  16.0 0.0 copy-done.6
  16.0 0.0 copy-start.3
  16.0 1.6 %copy-done.3 = f32[2048,256]{1,0:T(8,128)S(1)} copy-done((f32[2048,256]{1,0:T(8,128)S(1)}, f32[2048,256]{1,0:T(8,128)}, u32[]{:S(2)}) %copy-start.3) | copy-done | bytes 2097176
  17.6 0.0 copy-start.4
  17.6 3.2 %filter_spectra.1.filt_hbm = f32[2,8,256,128]{3,2,1,0:T(8,128)} custom-call(s32[1]{0:T(128)} %bitcast.4.place_ref, f32[2048,256]{1,0:T(8,128)S(1)} %copy-done.3, bf16[512,256]{1,0:T(8,128)(2,1)S(1)} %copy-done.5, bf16[512,256]{1,0:T(8,128)(2,1)S(1)} %copy-done.6), custom_call_target="tpu_custom_call" | custom-call | tf_op jit(solution)/shard_map/filter_spectra/pallas_call | solution.py:399
  20.8 19.8 %all-to-all-done.arrived_ref = bf16[64,2,64,128]{3,2,1,0:T(8,128)(2,1)S(1)} async-done(((bf16[64,2,64,128]{3,2,1,0:T(8,128)(2,1)}), bf16[64,2,64,128]{3,2,1,0:T(8,128)(2,1)S(1)}, u32[]{:S(2)}, u32[]{:S(2)}) %all-to-all-start) | async-done | bytes 2097184 | tf_op jit(solution)/shard_map/all_to_all | solution.py:394
  40.6 0.0 copy-done.4
  40.6 4.9 %filter_terms.1 = (bf16[1024,128]{1,0:T(8,128)(2,1)S(1)}, f32[8,512,256]{2,1,0:T(8,128)S(1)}, f32[8,512,256]{2,1,0:T(8,128)S(1)}, f32[2,8,256,128]{3,2,1,0:T(8,128)S(1)}) custom-call(bf16[64,2,64,128]{3,2,1,0:T(8,128)(2,1)S(1)} %all-to-all-done.arrived_ref, bf16[512,256]{1,0:T(8,128)(2,1)S(1)} %copy-done.5, bf16[256,512]{1,0:T(8,128)(2,1)S(1)} %copy-done.4, ...), custom_call_target="tpu_custom_call" | custom-call | tf_op jit(solution)/shard_map/filter_terms/pallas_call | solution.py:420
  45.5 3.4 %collective-permute-start = (bf16[1024,128]{1,0:T(8,128)(2,1)S(1)}, bf16[1024,128]{1,0:T(8,128)(2,1)S(1)}, u32[]{:S(2)}, u32[]{:S(2)}) collective-permute-start(bf16[1024,128]{1,0:T(8,128)(2,1)S(1)} %get-tuple-element.16), channel_id=1, source_target_pairs={{0,64},{16,80},{32,96},{48,112},{64,0},{80,16},{96,32},{112,48},{1... | collective-permute-start | bytes 786440 | tf_op jit(solution)/shard_map/ppermute | solution.py:452
  48.9 7.0 %convolve.1 = bf16[64,2,64,128]{3,2,1,0:T(8,128)(2,1)} custom-call(f32[8,512,256]{2,1,0:T(8,128)S(1)} %get-tuple-element.13.value_ref, f32[8,512,256]{2,1,0:T(8,128)S(1)} %get-tuple-element.14.grad_ref, f32[2,8,256,128]{3,2,1,0:T(8,128)S(1)} %get-tuple-element.15.filt_ref, bf16[256,512]{1,0:T(8,128)(2,1)S(1)} %copy-done.4), custom_call_target="tpu_custom_call" | custom-call | tf_op jit(solution)/shard_map/convolve/pallas_call | solution.py:438
  55.9 0.0 collective-permute-done
  55.9 0.1 add_convert_fusion.own_ref
  56.0 0.0 copy-start
  56.0 8.9 %all-to-all-start.1 = ((bf16[64,2,64,128]{3,2,1,0:T(8,128)(2,1)}), bf16[64,2,64,128]{3,2,1,0:T(8,128)(2,1)S(1)}, u32[]{:S(2)}, u32[]{:S(2)}) async-start(bf16[64,2,64,128]{3,2,1,0:T(8,128)(2,1)} %convolve.1), calls=%async_computation.1 | async-start | bytes 4194304 | tf_op jit(solution)/shard_map/all_to_all | solution.py:394
  64.9 0.4 collective-permute-start.3
  65.3 1.8 %collective-permute-start.2 = (bf16[1024,128]{1,0:T(8,128)(2,1)S(1)}, bf16[1024,128]{1,0:T(8,128)(2,1)}, u32[]{:S(2)}, u32[]{:S(2)}) collective-permute-start(bf16[1024,128]{1,0:T(8,128)(2,1)S(1)} %add_convert_fusion.own_ref), channel_id=1, source_target_pairs={{0,48},{16,0},{32,16},{48,32},{64,112},{80,64},{96,80},{112,96},{1... | collective-permute-start | bytes 786440 | tf_op jit(solution)/shard_map/ppermute | solution.py:458
  67.1 0.0 collective-permute-start.1
  67.1 22.6 %all-to-all-done.1.ret_ref = bf16[64,2,64,128]{3,2,1,0:T(8,128)(2,1)S(1)} async-done(((bf16[64,2,64,128]{3,2,1,0:T(8,128)(2,1)}), bf16[64,2,64,128]{3,2,1,0:T(8,128)(2,1)S(1)}, u32[]{:S(2)}, u32[]{:S(2)}) %all-to-all-start.1) | async-done | bytes 2097184 | tf_op jit(solution)/shard_map/all_to_all | solution.py:394
  89.6 0.0 copy-done
  89.6 0.0 copy-start.1
  89.7 1.2 %copy-done.1 = bf16[1,128,4096]{2,1,0:T(8,128)(2,1)S(1)} copy-done((bf16[1,128,4096]{2,1,0:T(8,128)(2,1)S(1)}, bf16[1,128,4096]{2,1,0:T(8,128)(2,1)}, u32[]{:S(2)}) %copy-start.1) | copy-done | bytes 1048600
  90.9 0.0 copy-start.2
  90.9 1.2 %copy-done.2 = bf16[1,128,4096]{2,1,0:T(8,128)(2,1)S(1)} copy-done((bf16[1,128,4096]{2,1,0:T(8,128)(2,1)S(1)}, bf16[1,128,4096]{2,1,0:T(8,128)(2,1)}, u32[]{:S(2)}) %copy-start.2) | copy-done | bytes 1048600
  92.1 2.1 %products.1 = (bf16[128,4096]{1,0:T(8,128)(2,1)}, bf16[128,4096]{1,0:T(8,128)(2,1)}, bf16[128,4096]{1,0:T(8,128)(2,1)}) custom-call(bf16[64,2,64,128]{3,2,1,0:T(8,128)(2,1)S(1)} %all-to-all-done.1.ret_ref, bf16[128,4096]{1,0:T(8,128)(2,1)S(1)} %bitcast.9, bf16[128,4096]{1,0:T(8,128)(2,1)S(1)} %bitcast.11, bf16[128,4096]{1,0:T(8,128)(2,1)S(1)} %bitcast.13), custom_call_target="tpu_custom_call" | custom-call | tf_op jit(solution)/shard_map/products/pallas_call | solution.py:466
  94.2 0.6 collective-permute-done.3.far_ref
  94.8 4.3 %collective-permute-done.2.down_ref = bf16[1024,128]{1,0:T(8,128)(2,1)} collective-permute-done((bf16[1024,128]{1,0:T(8,128)(2,1)S(1)}, bf16[1024,128]{1,0:T(8,128)(2,1)}, u32[]{:S(2)}, u32[]{:S(2)}) %collective-permute-start.2) | collective-permute-done | bytes 262176 | tf_op jit(solution)/shard_map/ppermute | solution.py:458
  99.2 0.4 collective-permute-done.1.up_ref
  99.5 2.7 %spread.1 = f32[2048,256]{1,0:T(8,128)} custom-call(s32[1]{0:T(128)} %bitcast.4.place_ref, bf16[1024,128]{1,0:T(8,128)(2,1)S(1)} %add_convert_fusion.own_ref, bf16[1024,128]{1,0:T(8,128)(2,1)} %collective-permute-done.1.up_ref, bf16[1024,128]{1,0:T(8,128)(2,1)} %collective-permute-done.2.down_ref, bf16[1024,128]{1,0:T(8,128)(2,1)} %collective-permute-done.3.far_ref, ...), custom_call_target="tpu_custom_call" | custom-call | tf_op jit(solution)/shard_map/spread/pallas_call | solution.py:475
Async XLA Ops:
  4.1 11.9 %copy-start.5 = (bf16[512,256]{1,0:T(8,128)(2,1)S(1)}, bf16[512,256]{1,0:T(8,128)(2,1)}, u32[]{:S(2)}) copy-start(bf16[512,256]{1,0:T(8,128)(2,1)} %constant.17.clone.upper_ref.forward_ref) | copy-start | bytes 786436
  4.1 11.9 %copy-start.6 = (bf16[512,256]{1,0:T(8,128)(2,1)S(1)}, bf16[512,256]{1,0:T(8,128)(2,1)}, u32[]{:S(2)}) copy-start(bf16[512,256]{1,0:T(8,128)(2,1)} %constant.18.clone.lower_ref) | copy-start | bytes 786436
  4.1 36.5 %all-to-all-start = ((bf16[64,2,64,128]{3,2,1,0:T(8,128)(2,1)}), bf16[64,2,64,128]{3,2,1,0:T(8,128)(2,1)S(1)}, u32[]{:S(2)}, u32[]{:S(2)}) async-start(bf16[64,2,64,128]{3,2,1,0:T(8,128)(2,1)} %gate.1), calls=%async_computation | async-start | bytes 4194304 | tf_op jit(solution)/shard_map/all_to_all | solution.py:394
  16.0 1.6 %copy-start.3 = (f32[2048,256]{1,0:T(8,128)S(1)}, f32[2048,256]{1,0:T(8,128)}, u32[]{:S(2)}) copy-start(f32[2048,256]{1,0:T(8,128)} %taps_ref.1) | copy-start | bytes 6291460
  17.6 23.0 %copy-start.4 = (bf16[256,512]{1,0:T(8,128)(2,1)S(1)}, bf16[256,512]{1,0:T(8,128)(2,1)}, u32[]{:S(2)}) copy-start(bf16[256,512]{1,0:T(8,128)(2,1)} %constant.19.clone.inverse_ref) | copy-start | bytes 786436
  45.5 10.4 %collective-permute-start = (bf16[1024,128]{1,0:T(8,128)(2,1)S(1)}, bf16[1024,128]{1,0:T(8,128)(2,1)S(1)}, u32[]{:S(2)}, u32[]{:S(2)}) collective-permute-start(bf16[1024,128]{1,0:T(8,128)(2,1)S(1)} %get-tuple-element.16), channel_id=1, source_target_pairs={{0,64},{16,80},{32,96},{48,112},{64,0},{80,16},{96,32},{112,48},{1... | collective-permute-start | bytes 786440 | tf_op jit(solution)/shard_map/ppermute | solution.py:452
  56.0 33.7 %copy-start = (bf16[1,128,4096]{2,1,0:T(8,128)(2,1)S(1)}, bf16[1,128,4096]{2,1,0:T(8,128)(2,1)}, u32[]{:S(2)}) copy-start(bf16[1,128,4096]{2,1,0:T(8,128)(2,1)} %param.9) | copy-start | bytes 3145732
  56.0 33.7 %all-to-all-start.1 = ((bf16[64,2,64,128]{3,2,1,0:T(8,128)(2,1)}), bf16[64,2,64,128]{3,2,1,0:T(8,128)(2,1)S(1)}, u32[]{:S(2)}, u32[]{:S(2)}) async-start(bf16[64,2,64,128]{3,2,1,0:T(8,128)(2,1)} %convolve.1), calls=%async_computation.1 | async-start | bytes 4194304 | tf_op jit(solution)/shard_map/all_to_all | solution.py:394
  64.9 29.9 %collective-permute-start.3 = (bf16[1024,128]{1,0:T(8,128)(2,1)S(1)}, bf16[1024,128]{1,0:T(8,128)(2,1)}, u32[]{:S(2)}, u32[]{:S(2)}) collective-permute-start(bf16[1024,128]{1,0:T(8,128)(2,1)S(1)} %add_convert_fusion.own_ref), channel_id=1, source_target_pairs={{0,32},{16,48},{32,0},{48,16},{64,96},{80,112},{96,64},{112,80},{1... | collective-permute-start | bytes 786440 | tf_op jit(solution)/shard_map/ppermute | solution.py:458
  65.3 33.9 %collective-permute-start.2 = (bf16[1024,128]{1,0:T(8,128)(2,1)S(1)}, bf16[1024,128]{1,0:T(8,128)(2,1)}, u32[]{:S(2)}, u32[]{:S(2)}) collective-permute-start(bf16[1024,128]{1,0:T(8,128)(2,1)S(1)} %add_convert_fusion.own_ref), channel_id=1, source_target_pairs={{0,48},{16,0},{32,16},{48,32},{64,112},{80,64},{96,80},{112,96},{1... | collective-permute-start | bytes 786440 | tf_op jit(solution)/shard_map/ppermute | solution.py:458
  67.1 32.5 %collective-permute-start.1 = (bf16[1024,128]{1,0:T(8,128)(2,1)S(1)}, bf16[1024,128]{1,0:T(8,128)(2,1)}, u32[]{:S(2)}, u32[]{:S(2)}) collective-permute-start(bf16[1024,128]{1,0:T(8,128)(2,1)S(1)} %add_convert_fusion.own_ref), channel_id=1, source_target_pairs={{0,16},{16,32},{32,48},{48,0},{64,80},{80,96},{96,112},{112,64},{1... | collective-permute-start | bytes 786440 | tf_op jit(solution)/shard_map/ppermute | solution.py:458
  89.6 1.2 %copy-start.1 = (bf16[1,128,4096]{2,1,0:T(8,128)(2,1)S(1)}, bf16[1,128,4096]{2,1,0:T(8,128)(2,1)}, u32[]{:S(2)}) copy-start(bf16[1,128,4096]{2,1,0:T(8,128)(2,1)} %param.10) | copy-start | bytes 3145732
  90.9 1.2 %copy-start.2 = (bf16[1,128,4096]{2,1,0:T(8,128)(2,1)S(1)}, bf16[1,128,4096]{2,1,0:T(8,128)(2,1)}, u32[]{:S(2)}) copy-start(bf16[1,128,4096]{2,1,0:T(8,128)(2,1)} %param.11) | copy-start | bytes 3145732

commit v6 on v5

--- a/solution.py
+++ b/solution.py
@@ -17,6 +17,7 @@
 BF16 = jnp.bfloat16
 TILE = 32
 CHUNKS = 4
+SPREAD_CHUNKS = 8
 VMEM_LIMIT = 24 * 1024 * 1024
 SMALL_LIMIT = 12 * 1024 * 1024
 
@@ -334,12 +335,12 @@
 ):
     count = held_ref.shape[0]
     rows = held_ref.shape[1]
-    step = rows // CHUNKS
+    step = rows // SPREAD_CHUNKS
     place = place_ref[0]
     for ref, shift in ((own_ref, 0), (up_ref, 1), (down_ref, 3), (far_ref, 2)):
         held_ref[lax.rem(place + count - shift, count)] = ref[...]
     stores = []
-    for chunk in range(CHUNKS):
+    for chunk in range(SPREAD_CHUNKS):
         part = pl.ds(chunk * step, step)
         for pair in range(2):
             lanes = pl.ds(pair * LANES, LANES)
@@ -480,7 +481,7 @@
         scratch_shapes=[
             pltpu.VMEM((y_count, length // 2, LANES), BF16),
             pltpu.VMEM((length, 2 * LANES), F32),
-            pltpu.SemaphoreType.DMA((2, CHUNKS)),
+            pltpu.SemaphoreType.DMA((2, SPREAD_CHUNKS)),
         ],
         compiler_params=pltpu.CompilerParams(vmem_limit_bytes=SMALL_LIMIT),
         name="spread",

time: 103 us -> 103 us (level)
  no operation moved by 1% of the time
where the time goes in v6:
time: 103 us; the launch traced here: 102 us
  waiting for transfers between devices  47.6 us (46%)
  starting transfers between devices  26.3 us (26%)
  Pallas kernels  23.4 us (23%)
  local copies, waits for them, and re-layouts  4.06 us (4%)
    all_to_all x2, waiting for transfers between devices, exchange(): lax.all_to_all(array, ('seq', 'ctx'), 0, 0, tiled=True, axis_index_groups...  42.3 us
    all_to_all x2, starting transfers between devices, exchange(): lax.all_to_all(array, ('seq', 'ctx'), 0, 0, tiled=True, axis_index_groups...  20.8 us
    pallas_call x1, Pallas kernels, local(): pl.pallas_call(functools.partial(conv_kernel, slots=place_of), in_specs=[...  6.99 us
    ppermute x3, waiting for transfers between devices, local(): lax.ppermute(summed, 'seq', [(s, s // y_count * y_count + (s + shift) % y...  5.31 us
    pallas_call x1, Pallas kernels, local(): pl.pallas_call(functools.partial(cross_kernel, slots=place_of), in_specs=...  4.93 us
    unnamed x14, local copies, waits for them, and re-layouts  4.06 us
    pallas_call x1, Pallas kernels, local(): pl.pallas_call(functools.partial(gate_kernel, slots=place_of), in_specs=[...  3.42 us
    ppermute x1, starting transfers between devices, local(): lax.ppermute(part_grad, 'seq', [(s, (s + y_count) % seq_count) for s in r...  3.38 us
  transfers between devices with their start and end apart: 6, of which 5 were waited for; matrix products, arithmetic and copies ran while one was open for 0% of the time, Pallas kernels for 12%

profile of v6, /device:TPU:1, one launch (start us, length us, event | category | flops | bytes accessed | tf_op | source)
XLA Modules:
  0.0 102.3 jit_solution(15058591603676360762)
XLA Ops:
  0.6 3.4 %gate.1 = bf16[64,2,64,128]{3,2,1,0:T(8,128)(2,1)} custom-call(bf16[128,4096]{1,0:T(8,128)(2,1)} %bitcast.15, bf16[128,4096]{1,0:T(8,128)(2,1)} %bitcast.8, bf16[128,4096]{1,0:T(8,128)(2,1)} %bitcast.10, bf16[128,4096]{1,0:T(8,128)(2,1)} %bitcast.12), custom_call_target="tpu_custom_call" | custom-call | tf_op jit(solution)/shard_map/gate/pallas_call | solution.py:379
  4.1 0.0 copy-start.5
  4.1 0.0 copy-start.6
  4.1 11.8 %all-to-all-start = ((bf16[64,2,64,128]{3,2,1,0:T(8,128)(2,1)}), bf16[64,2,64,128]{3,2,1,0:T(8,128)(2,1)S(1)}, u32[]{:S(2)}, u32[]{:S(2)}) async-start(bf16[64,2,64,128]{3,2,1,0:T(8,128)(2,1)} %gate.1), calls=%async_computation | async-start | bytes 4194304 | tf_op jit(solution)/shard_map/all_to_all | solution.py:395
  15.9 0.0 copy-done.5
  16.0 0.0 copy-done.6
  16.0 0.0 copy-start.3
  16.0 1.6 %copy-done.3 = f32[2048,256]{1,0:T(8,128)S(1)} copy-done((f32[2048,256]{1,0:T(8,128)S(1)}, f32[2048,256]{1,0:T(8,128)}, u32[]{:S(2)}) %copy-start.3) | copy-done | bytes 2097176
  17.6 0.0 copy-start.4
  17.6 3.2 %filter_spectra.1.filt_hbm = f32[2,8,256,128]{3,2,1,0:T(8,128)} custom-call(s32[1]{0:T(128)} %bitcast.4.place_ref, f32[2048,256]{1,0:T(8,128)S(1)} %copy-done.3, bf16[512,256]{1,0:T(8,128)(2,1)S(1)} %copy-done.5, bf16[512,256]{1,0:T(8,128)(2,1)S(1)} %copy-done.6), custom_call_target="tpu_custom_call" | custom-call | tf_op jit(solution)/shard_map/filter_spectra/pallas_call | solution.py:400
  20.8 19.8 %all-to-all-done.arrived_ref = bf16[64,2,64,128]{3,2,1,0:T(8,128)(2,1)S(1)} async-done(((bf16[64,2,64,128]{3,2,1,0:T(8,128)(2,1)}), bf16[64,2,64,128]{3,2,1,0:T(8,128)(2,1)S(1)}, u32[]{:S(2)}, u32[]{:S(2)}) %all-to-all-start) | async-done | bytes 2097184 | tf_op jit(solution)/shard_map/all_to_all | solution.py:395
  40.6 0.0 copy-done.4
  40.6 4.9 %filter_terms.1 = (bf16[1024,128]{1,0:T(8,128)(2,1)S(1)}, f32[8,512,256]{2,1,0:T(8,128)S(1)}, f32[8,512,256]{2,1,0:T(8,128)S(1)}, f32[2,8,256,128]{3,2,1,0:T(8,128)S(1)}) custom-call(bf16[64,2,64,128]{3,2,1,0:T(8,128)(2,1)S(1)} %all-to-all-done.arrived_ref, bf16[512,256]{1,0:T(8,128)(2,1)S(1)} %copy-done.5, bf16[256,512]{1,0:T(8,128)(2,1)S(1)} %copy-done.4, ...), custom_call_target="tpu_custom_call" | custom-call | tf_op jit(solution)/shard_map/filter_terms/pallas_call | solution.py:421
  45.5 3.4 %collective-permute-start = (bf16[1024,128]{1,0:T(8,128)(2,1)S(1)}, bf16[1024,128]{1,0:T(8,128)(2,1)S(1)}, u32[]{:S(2)}, u32[]{:S(2)}) collective-permute-start(bf16[1024,128]{1,0:T(8,128)(2,1)S(1)} %get-tuple-element.16), channel_id=1, source_target_pairs={{0,64},{16,80},{32,96},{48,112},{64,0},{80,16},{96,32},{112,48},{1... | collective-permute-start | bytes 786440 | tf_op jit(solution)/shard_map/ppermute | solution.py:453
  48.9 7.0 %convolve.1 = bf16[64,2,64,128]{3,2,1,0:T(8,128)(2,1)} custom-call(f32[8,512,256]{2,1,0:T(8,128)S(1)} %get-tuple-element.13.value_ref, f32[8,512,256]{2,1,0:T(8,128)S(1)} %get-tuple-element.14.grad_ref, f32[2,8,256,128]{3,2,1,0:T(8,128)S(1)} %get-tuple-element.15.filt_ref, bf16[256,512]{1,0:T(8,128)(2,1)S(1)} %copy-done.4), custom_call_target="tpu_custom_call" | custom-call | tf_op jit(solution)/shard_map/convolve/pallas_call | solution.py:439
  55.9 0.0 collective-permute-done
  55.9 0.1 add_convert_fusion.own_ref
  56.0 0.0 copy-start
  56.0 8.9 %all-to-all-start.1 = ((bf16[64,2,64,128]{3,2,1,0:T(8,128)(2,1)}), bf16[64,2,64,128]{3,2,1,0:T(8,128)(2,1)S(1)}, u32[]{:S(2)}, u32[]{:S(2)}) async-start(bf16[64,2,64,128]{3,2,1,0:T(8,128)(2,1)} %convolve.1), calls=%async_computation.1 | async-start | bytes 4194304 | tf_op jit(solution)/shard_map/all_to_all | solution.py:395
  64.9 0.4 collective-permute-start.3
  65.3 1.8 %collective-permute-start.2 = (bf16[1024,128]{1,0:T(8,128)(2,1)S(1)}, bf16[1024,128]{1,0:T(8,128)(2,1)}, u32[]{:S(2)}, u32[]{:S(2)}) collective-permute-start(bf16[1024,128]{1,0:T(8,128)(2,1)S(1)} %add_convert_fusion.own_ref), channel_id=1, source_target_pairs={{0,48},{16,0},{32,16},{48,32},{64,112},{80,64},{96,80},{112,96},{1... | collective-permute-start | bytes 786440 | tf_op jit(solution)/shard_map/ppermute | solution.py:459
  67.1 0.0 collective-permute-start.1
  67.1 22.6 %all-to-all-done.1.ret_ref = bf16[64,2,64,128]{3,2,1,0:T(8,128)(2,1)S(1)} async-done(((bf16[64,2,64,128]{3,2,1,0:T(8,128)(2,1)}), bf16[64,2,64,128]{3,2,1,0:T(8,128)(2,1)S(1)}, u32[]{:S(2)}, u32[]{:S(2)}) %all-to-all-start.1) | async-done | bytes 2097184 | tf_op jit(solution)/shard_map/all_to_all | solution.py:395
  89.6 0.0 copy-done
  89.6 0.0 copy-start.1
  89.7 1.2 %copy-done.1 = bf16[1,128,4096]{2,1,0:T(8,128)(2,1)S(1)} copy-done((bf16[1,128,4096]{2,1,0:T(8,128)(2,1)S(1)}, bf16[1,128,4096]{2,1,0:T(8,128)(2,1)}, u32[]{:S(2)}) %copy-start.1) | copy-done | bytes 1048600
  90.9 0.0 copy-start.2
  90.9 1.2 %copy-done.2 = bf16[1,128,4096]{2,1,0:T(8,128)(2,1)S(1)} copy-done((bf16[1,128,4096]{2,1,0:T(8,128)(2,1)S(1)}, bf16[1,128,4096]{2,1,0:T(8,128)(2,1)}, u32[]{:S(2)}) %copy-start.2) | copy-done | bytes 1048600
  92.1 2.1 %products.1 = (bf16[128,4096]{1,0:T(8,128)(2,1)}, bf16[128,4096]{1,0:T(8,128)(2,1)}, bf16[128,4096]{1,0:T(8,128)(2,1)}) custom-call(bf16[64,2,64,128]{3,2,1,0:T(8,128)(2,1)S(1)} %all-to-all-done.1.ret_ref, bf16[128,4096]{1,0:T(8,128)(2,1)S(1)} %bitcast.9, bf16[128,4096]{1,0:T(8,128)(2,1)S(1)} %bitcast.11, bf16[128,4096]{1,0:T(8,128)(2,1)S(1)} %bitcast.13), custom_call_target="tpu_custom_call" | custom-call | tf_op jit(solution)/shard_map/products/pallas_call | solution.py:467
  94.2 0.6 collective-permute-done.3.far_ref
  94.8 4.3 %collective-permute-done.2.down_ref = bf16[1024,128]{1,0:T(8,128)(2,1)} collective-permute-done((bf16[1024,128]{1,0:T(8,128)(2,1)S(1)}, bf16[1024,128]{1,0:T(8,128)(2,1)}, u32[]{:S(2)}, u32[]{:S(2)}) %collective-permute-start.2) | collective-permute-done | bytes 262176 | tf_op jit(solution)/shard_map/ppermute | solution.py:459
  99.2 0.4 collective-permute-done.1.up_ref
  99.5 2.7 %spread.1 = f32[2048,256]{1,0:T(8,128)} custom-call(s32[1]{0:T(128)} %bitcast.4.place_ref, bf16[1024,128]{1,0:T(8,128)(2,1)S(1)} %add_convert_fusion.own_ref, bf16[1024,128]{1,0:T(8,128)(2,1)} %collective-permute-done.1.up_ref, bf16[1024,128]{1,0:T(8,128)(2,1)} %collective-permute-done.2.down_ref, bf16[1024,128]{1,0:T(8,128)(2,1)} %collective-permute-done.3.far_ref, ...), custom_call_target="tpu_custom_call" | custom-call | tf_op jit(solution)/shard_map/spread/pallas_call | solution.py:476
Async XLA Ops:
  4.1 11.9 %copy-start.5 = (bf16[512,256]{1,0:T(8,128)(2,1)S(1)}, bf16[512,256]{1,0:T(8,128)(2,1)}, u32[]{:S(2)}) copy-start(bf16[512,256]{1,0:T(8,128)(2,1)} %constant.17.clone.upper_ref.forward_ref) | copy-start | bytes 786436
  4.1 11.9 %copy-start.6 = (bf16[512,256]{1,0:T(8,128)(2,1)S(1)}, bf16[512,256]{1,0:T(8,128)(2,1)}, u32[]{:S(2)}) copy-start(bf16[512,256]{1,0:T(8,128)(2,1)} %constant.18.clone.lower_ref) | copy-start | bytes 786436
  4.1 36.5 %all-to-all-start = ((bf16[64,2,64,128]{3,2,1,0:T(8,128)(2,1)}), bf16[64,2,64,128]{3,2,1,0:T(8,128)(2,1)S(1)}, u32[]{:S(2)}, u32[]{:S(2)}) async-start(bf16[64,2,64,128]{3,2,1,0:T(8,128)(2,1)} %gate.1), calls=%async_computation | async-start | bytes 4194304 | tf_op jit(solution)/shard_map/all_to_all | solution.py:395
  16.0 1.6 %copy-start.3 = (f32[2048,256]{1,0:T(8,128)S(1)}, f32[2048,256]{1,0:T(8,128)}, u32[]{:S(2)}) copy-start(f32[2048,256]{1,0:T(8,128)} %taps_ref.1) | copy-start | bytes 6291460
  17.6 23.0 %copy-start.4 = (bf16[256,512]{1,0:T(8,128)(2,1)S(1)}, bf16[256,512]{1,0:T(8,128)(2,1)}, u32[]{:S(2)}) copy-start(bf16[256,512]{1,0:T(8,128)(2,1)} %constant.19.clone.inverse_ref) | copy-start | bytes 786436
  45.5 10.4 %collective-permute-start = (bf16[1024,128]{1,0:T(8,128)(2,1)S(1)}, bf16[1024,128]{1,0:T(8,128)(2,1)S(1)}, u32[]{:S(2)}, u32[]{:S(2)}) collective-permute-start(bf16[1024,128]{1,0:T(8,128)(2,1)S(1)} %get-tuple-element.16), channel_id=1, source_target_pairs={{0,64},{16,80},{32,96},{48,112},{64,0},{80,16},{96,32},{112,48},{1... | collective-permute-start | bytes 786440 | tf_op jit(solution)/shard_map/ppermute | solution.py:453
  56.0 33.7 %copy-start = (bf16[1,128,4096]{2,1,0:T(8,128)(2,1)S(1)}, bf16[1,128,4096]{2,1,0:T(8,128)(2,1)}, u32[]{:S(2)}) copy-start(bf16[1,128,4096]{2,1,0:T(8,128)(2,1)} %param.9) | copy-start | bytes 3145732
  56.0 33.7 %all-to-all-start.1 = ((bf16[64,2,64,128]{3,2,1,0:T(8,128)(2,1)}), bf16[64,2,64,128]{3,2,1,0:T(8,128)(2,1)S(1)}, u32[]{:S(2)}, u32[]{:S(2)}) async-start(bf16[64,2,64,128]{3,2,1,0:T(8,128)(2,1)} %convolve.1), calls=%async_computation.1 | async-start | bytes 4194304 | tf_op jit(solution)/shard_map/all_to_all | solution.py:395
  64.9 29.9 %collective-permute-start.3 = (bf16[1024,128]{1,0:T(8,128)(2,1)S(1)}, bf16[1024,128]{1,0:T(8,128)(2,1)}, u32[]{:S(2)}, u32[]{:S(2)}) collective-permute-start(bf16[1024,128]{1,0:T(8,128)(2,1)S(1)} %add_convert_fusion.own_ref), channel_id=1, source_target_pairs={{0,32},{16,48},{32,0},{48,16},{64,96},{80,112},{96,64},{112,80},{1... | collective-permute-start | bytes 786440 | tf_op jit(solution)/shard_map/ppermute | solution.py:459
  65.3 33.9 %collective-permute-start.2 = (bf16[1024,128]{1,0:T(8,128)(2,1)S(1)}, bf16[1024,128]{1,0:T(8,128)(2,1)}, u32[]{:S(2)}, u32[]{:S(2)}) collective-permute-start(bf16[1024,128]{1,0:T(8,128)(2,1)S(1)} %add_convert_fusion.own_ref), channel_id=1, source_target_pairs={{0,48},{16,0},{32,16},{48,32},{64,112},{80,64},{96,80},{112,96},{1... | collective-permute-start | bytes 786440 | tf_op jit(solution)/shard_map/ppermute | solution.py:459
  67.1 32.5 %collective-permute-start.1 = (bf16[1024,128]{1,0:T(8,128)(2,1)S(1)}, bf16[1024,128]{1,0:T(8,128)(2,1)}, u32[]{:S(2)}, u32[]{:S(2)}) collective-permute-start(bf16[1024,128]{1,0:T(8,128)(2,1)S(1)} %add_convert_fusion.own_ref), channel_id=1, source_target_pairs={{0,16},{16,32},{32,48},{48,0},{64,80},{80,96},{96,112},{112,64},{1... | collective-permute-start | bytes 786440 | tf_op jit(solution)/shard_map/ppermute | solution.py:459
  89.6 1.2 %copy-start.1 = (bf16[1,128,4096]{2,1,0:T(8,128)(2,1)S(1)}, bf16[1,128,4096]{2,1,0:T(8,128)(2,1)}, u32[]{:S(2)}) copy-start(bf16[1,128,4096]{2,1,0:T(8,128)(2,1)} %param.10) | copy-start | bytes 3145732
  90.9 1.2 %copy-start.2 = (bf16[1,128,4096]{2,1,0:T(8,128)(2,1)S(1)}, bf16[1,128,4096]{2,1,0:T(8,128)(2,1)}, u32[]{:S(2)}) copy-start(bf16[1,128,4096]{2,1,0:T(8,128)(2,1)} %param.11) | copy-start | bytes 3145732
